TPU v7x, 32 devices: a whole 2x2x4 slice. The times are simulated.
32 devices in a mesh: ctx: 16 (over z, x, core), ch: 2 (over y).
Axes of the slice: x: 2, y: 2, z: 4, core: 2. Of those that a mesh axis runs over, the one named last changes fastest.
Arguments:
- hidden: bfloat16 [4096, 2048], P('ctx', 'ch'), may hold values from -6 to 6
- channel_perm: int32 [2048], replicated, may hold values from 0 to 2047, each once
- input_weight: bfloat16 [2048, 2048], P(None, 'ch'), may hold values from -0.125 to 0.125
- state_weight: bfloat16 [2048, 32], replicated, may hold values from -0.03125 to 0.03125
- step_weight: bfloat16 [2048, 32], P(None, 'ch'), may hold values from -0.25 to 0.25
- step_bias: float32 [32], P('ch'), may hold values from -5 to -1
- decay_log: float32 [32], P('ch'), may hold values from -6 to 2
- filter_taps: float32 [4, 2048], P(None, 'ch'), may hold values from -3 to 3
- skip_gain: float32 [2048], P('ch'), may hold values from 0.5 to 1.5
- output_weight: bfloat16 [2048, 2048], P('ch'), may hold values from -0.125 to 0.125
- cotangent: bfloat16 [4096, 2048], P('ctx', 'ch'), may hold values from -0.119628906 to 0.119628906
Outputs:
- layer_out: bfloat16 [4096, 2048], P('ctx', 'ch')
- grad_input_weight: float32 [2048, 2048], P(None, 'ch')
- grad_filter: float32 [4, 2048], P(None, 'ch')
- grad_skip: float32 [2048], P('ch')
Inputs may be any that keep to these rules, and one draw needn't show every extreme that they name: channel_perm holds each channel number once.
All inputs are finite; a program needn't handle non-finite values.
Results may differ from a plain program's by a relative error of at most 0.012.
Values may be sent and summed in bfloat16 or wider, within the bound.
A program may use at most 128 MiB of HBM per device.

v0:
```python
import functools

import jax
import jax.numpy as jnp
from jax import lax
from jax.experimental import pallas as pl
from jax.experimental.pallas import tpu as pltpu
from jax.sharding import PartitionSpec as P

EXACT = lax.Precision.HIGHEST
F32, BF16 = jnp.float32, jnp.bfloat16
RIM = 16


def dot(a, b, dims=((1,), (0,)), precision=None):
    return lax.dot_general(
        a, b, (dims, ((), ())), preferred_element_type=F32, precision=precision
    )


def shifted(x, taps_at, branch, length):
    start = RIM - taps_at if branch == 0 else taps_at
    return x[start : start + length]


def head_lanes(per_head_col, first, group, depth, length):
    lane = lax.broadcasted_iota(jnp.int32, (length, group * depth), 1)
    value = jnp.broadcast_to(per_head_col[:, first : first + 1], lane.shape)
    for extra in range(1, group):
        value = jnp.where(
            lane >= extra * depth,
            jnp.broadcast_to(per_head_col[:, first + extra : first + extra + 1], lane.shape),
            value,
        )
    return value


def local_kernel(
    depth, group, xf, xr, back, sizes, run, run_t, writes, reads, taps, gain,
    mixed, base, slopes, states, skip,
):
    length, width = back.shape
    row = lax.broadcasted_iota(jnp.int32, (length, length), 0)
    col = lax.broadcasted_iota(jnp.int32, (length, length), 1)
    scores = []
    for b in range(2):
        full = dot(reads[b], writes[b], ((1,), (1,)), EXACT)
        scores.append(jnp.where(row >= col if b == 0 else row <= col, full, 0.0))
    span = group * depth
    lane = lax.broadcasted_iota(jnp.int32, (length, span), 1)
    for q in range(width // span):
        cols = slice(q * span, (q + 1) * span)
        grad = back[:, cols]
        grad16 = grad.astype(BF16)
        total = None
        acts = None
        for b in range(2):
            x = (xf, xr)[b][:, cols].astype(F32)
            before = sum(
                taps[k : k + 1, cols] * shifted(x, k, b, length) for k in range(taps.shape[0])
            )
            sigma = jax.nn.sigmoid(before)
            act = before * sigma
            slope = sigma * (1.0 + before * (1.0 - sigma))
            size = head_lanes(sizes[b], q * group, group, depth, length)
            source = act * size
            source16 = source.astype(BF16)
            scan = adjoint = None
            for g in range(group):
                h = q * group + g
                spread = run[b, :, h : h + 1] - run_t[b, h : h + 1, :]
                decay = (jnp.exp(jnp.minimum(spread, 0.0)) * scores[b]).astype(BF16)
                one = dot(decay, source16)
                two = dot(decay, grad16, ((0,), (0,)))
                scan = one if g == 0 else jnp.where(lane >= g * depth, one, scan)
                adjoint = two if g == 0 else jnp.where(lane >= g * depth, two, adjoint)
            running = head_lanes(run[b], q * group, group, depth, length)
            end = running[length - 1 :] if b == 0 else running[:1]
            remain = jnp.exp(end - running)
            states[b, :, cols] = dot(
                writes[b].astype(BF16), (source * remain).astype(BF16), ((0,), (0,))
            ).astype(BF16)
            states[2 + b, :, cols] = dot(
                reads[b].astype(BF16), (grad * jnp.exp(running)).astype(BF16), ((0,), (0,))
            ).astype(BF16)
            base[b, :, cols] = (gain[:, cols] * grad + size * adjoint) * slope
            slopes[b, :, cols] = slope * size * remain
            total = scan if b == 0 else total + scan
            acts = act if b == 0 else acts + act
        mixed[:, cols] = total + gain[:, cols] * acts
        skip[:, cols] = jnp.sum(grad * acts, axis=0, keepdims=True)


def carry_kernel(
    depth, group, xf, xr, mixed_in, base, slopes, run, writes, reads, carried, taps,
    mixed, inner, edge, slope_edge, filt,
):
    length, width = mixed_in.shape
    span = group * depth
    taken = taps.shape[0]
    zeros = jnp.zeros((8, span), F32)
    for q in range(width // span):
        cols = slice(q * span, (q + 1) * span)
        total = mixed_in[:, cols]
        grads = [0.0] * taken
        for b in range(2):
            running = head_lanes(run[b], q * group, group, depth, length)
            total = total + jnp.exp(running) * dot(
                reads[b].astype(BF16), carried[b, :, cols].astype(BF16)
            )
            slope = base[b, :, cols] + slopes[b, :, cols] * dot(
                writes[b].astype(BF16), carried[2 + b, :, cols].astype(BF16)
            )
            x = (xf, xr)[b][:, cols].astype(F32)
            for k in range(taken):
                grads[k] = grads[k] + jnp.sum(
                    slope * shifted(x, k, b, length), axis=0, keepdims=True
                )
            if b == 0:
                longer = jnp.concatenate([slope, zeros], axis=0)
                parts = [longer[k : k + length] for k in range(taken)]
                slope_edge[b, :, cols] = slope[:8]
            else:
                longer = jnp.concatenate([zeros, slope], axis=0)
                parts = [longer[8 - k : 8 - k + length] for k in range(taken)]
                slope_edge[b, :, cols] = slope[length - 8 :]
            grad = sum(taps[k : k + 1, cols] * parts[k] for k in range(taken))
            inner[b * length : (b + 1) * length, cols] = grad.astype(BF16)
            edge[b, :, cols] = grad[length - 8 :] if b == 0 else grad[:8]
        mixed[:, cols] = total.astype(BF16)
        for k in range(taken):
            filt[k : k + 1, cols] = grads[k]


def vmem_call(body, shapes, *operands):
    spec = pl.BlockSpec(memory_space=pltpu.VMEM)
    return pl.pallas_call(
        body,
        out_shape=[jax.ShapeDtypeStruct(*s) for s in shapes],
        in_specs=[spec] * len(operands),
        out_specs=[spec] * len(shapes),
        compiler_params=pltpu.CompilerParams(vmem_limit_bytes=48 * 1024 * 1024),
    )(*operands)


def per_device(
    hidden, channel_perm, input_weight, state_weight, step_weight, step_bias, decay_log,
    filter_taps, skip_gain, output_weight, cotangent,
):
    length = hidden.shape[0]
    taken, width = filter_taps.shape
    heads = step_weight.shape[1]
    depth = width // heads
    group = max(1, 128 // depth)
    states = state_weight.shape[1] // 2
    model = input_weight.shape[0]
    count, me = lax.axis_size("ctx"), lax.axis_index("ctx")
    pair = lax.axis_size("ch") == 2
    side = lax.axis_index("ch")
    up = [(i, i + 1) for i in range(count - 1)]
    down = [(i + 1, i) for i in range(count - 1)]
    swap = [(0, 1), (1, 0)]

    def gathered(part):
        if not pair:
            return lax.all_gather(part, "ch", axis=1, tiled=True)
        other = lax.ppermute(part, "ch", swap)
        return jnp.where(
            side == 0,
            jnp.concatenate([part, other], 1),
            jnp.concatenate([other, part], 1),
        )

    embed = gathered(hidden)
    upstream = gathered(cotangent)
    onehot = (
        lax.broadcasted_iota(jnp.int32, (model, model), 0) == channel_perm[None, :]
    ).astype(BF16)
    both = jnp.concatenate([embed, dot(embed, onehot).astype(BF16)], 0)
    inner = dot(both, input_weight).astype(BF16)
    small = dot(both, jnp.concatenate([state_weight, step_weight], 1)).reshape(2, length, -1)
    fwd_rim = lax.ppermute(inner[length - RIM : length], "ctx", up)
    rev_rim = lax.ppermute(inner[length : length + RIM], "ctx", down)
    writes = small[:, :, :states]
    reads = small[:, :, states : 2 * states]
    sizes = jax.nn.softplus(small[:, :, 2 * states :] + step_bias[None, None, :])
    decays = -jnp.exp(decay_log)[None, None, :] * sizes
    totals = lax.all_gather(jnp.sum(decays, axis=1), "ctx")
    lower = jnp.tril(jnp.ones((length, length), F32))
    sums = jnp.stack([lower, lower.T])
    run = jnp.einsum("bts,bsh->bth", sums, decays, precision=EXACT)
    run_t = jnp.swapaxes(run, 1, 2)
    back = dot(upstream, output_weight, ((1,), (1,)))
    xf = jnp.concatenate([fwd_rim, inner[:length]], 0)
    xr = jnp.concatenate([inner[length:], rev_rim], 0)
    full = (length, width)
    mixed, base, slopes, ends, skip = vmem_call(
        functools.partial(local_kernel, depth, group),
        [
            (full, F32),
            ((2,) + full, F32),
            ((2,) + full, F32),
            ((4, states, width), BF16),
            ((1, width), F32),
        ],
        xf, xr, back, sizes, run, run_t, writes, reads, filter_taps, skip_gain[None, :],
    )
    pieces = lax.all_gather(ends, "ctx")
    j = jnp.arange(count)
    between = ((j[:, None] < j[None, :]) & (j[None, :] < me)) | (
        (j[None, :] < j[:, None]) & (j[None, :] > me)
    )
    weight = jnp.exp(jnp.einsum("ji,ibh->jbh", between.astype(F32), totals, precision=EXACT))
    earlier = jnp.where((j < me)[:, None], 1.0, 0.0)
    later = jnp.where((j > me)[:, None], 1.0, 0.0)
    kinds = jnp.stack(
        [
            weight[:, 0] * earlier,
            weight[:, 1] * later,
            weight[:, 0] * later,
            weight[:, 1] * earlier,
        ],
        axis=1,
    )
    kinds = jnp.repeat(kinds, depth, axis=2)
    carried = jnp.sum(kinds[:, :, None, :] * pieces.astype(F32), axis=0)
    mixed16, partial_grad, edge, slope_edge, filt = vmem_call(
        functools.partial(carry_kernel, depth, group),
        [
            (full, BF16),
            ((2 * length, width), BF16),
            ((2, 8, width), F32),
            ((2, 8, width), F32),
            ((taken, width), F32),
        ],
        xf, xr, mixed, base, slopes, run, writes, reads, carried, filter_taps,
    )
    fwd_after = lax.ppermute(slope_edge[0], "ctx", down)
    rev_after = lax.ppermute(slope_edge[1], "ctx", up)
    if pair:
        half = output_weight.shape[1] // 2
        theirs = lax.dynamic_slice_in_dim(output_weight, (1 - side) * half, half, 1)
        mine = lax.dynamic_slice_in_dim(output_weight, side * half, half, 1)
        arrived = lax.ppermute(dot(mixed16, theirs).astype(BF16), "ch", swap)
        layer_out = (dot(mixed16, mine) + arrived.astype(F32)).astype(BF16)
    else:
        layer_out = lax.psum_scatter(
            dot(mixed16, output_weight), "ch", scatter_dimension=1, tiled=True
        ).astype(BF16)
    zeros = jnp.zeros((8, width), F32)
    ahead = jnp.concatenate([zeros, fwd_after], 0)
    behind = jnp.concatenate([rev_after, zeros], 0)
    fwd_edge = edge[0] + sum(filter_taps[k][None] * ahead[k : k + 8] for k in range(taken))
    rev_edge = edge[1] + sum(
        filter_taps[k][None] * behind[8 - k : 16 - k] for k in range(taken)
    )
    grad_inner = jnp.concatenate(
        [
            partial_grad[: length - 8],
            fwd_edge.astype(BF16),
            rev_edge.astype(BF16),
            partial_grad[length + 8 :],
        ],
        0,
    )
    weight_local = dot(both, grad_inner, ((0,), (0,))).astype(BF16)
    tiny = lax.psum(jnp.concatenate([filt, skip], 0), "ctx")
    weight_sum = lax.psum_scatter(weight_local, "ctx", scatter_dimension=0, tiled=True)
    weight_grad = lax.all_gather(weight_sum, "ctx", axis=0, tiled=True).astype(F32)
    return (layer_out, weight_grad, tiny[:taken], tiny[taken])


def solution(mesh):
    placed = (
        P("ctx", "ch"), P(), P(None, "ch"), P(), P(None, "ch"), P("ch"), P("ch"),
        P(None, "ch"), P("ch"), P("ch", None), P("ctx", "ch"),
    )
    return jax.shard_map(
        per_device,
        mesh=mesh,
        in_specs=placed,
        out_specs=(P("ctx", "ch"), P(None, "ch"), P(None, "ch"), P("ch")),
        check_vma=False,
    )
```

profile of v0, /device:TPU:0, one launch (start us, length us, event | category | flops | bytes accessed | tf_op | source)
XLA Modules:
  0.0 270.3 jit_solution(15376590912088029361)
XLA Ops:
  7.2 3.0 %collective-permute-start = (bf16[256,1024]{1,0:T(8,128)(2,1)}, bf16[256,1024]{1,0:T(8,128)(2,1)S(1)}, u32[]{:S(2)}, u32[]{:S(2)}) collective-permute-start(bf16[256,1024]{1,0:T(8,128)(2,1)} %param.11), channel_id=1, source_target_pairs={{0,1},{1,0},{2,3},{3,2},{4,5},{5,4},{6,7},{7,6},{8,9},{9,8},{10,11... | collective-permute-start | bytes 1572872 | tf_op jit(solution)/shard_map/ppermute | solution.py:167
  10.4 0.7 exponential_negate_fusion
  11.0 12.2 %collective-permute-done = bf16[256,1024]{1,0:T(8,128)(2,1)S(1)} collective-permute-done((bf16[256,1024]{1,0:T(8,128)(2,1)}, bf16[256,1024]{1,0:T(8,128)(2,1)S(1)}, u32[]{:S(2)}, u32[]{:S(2)}) %collective-permute-start) | collective-permute-done | bytes 524320 | tf_op jit(solution)/shard_map/ppermute | solution.py:167
  23.2 1.6 maximum_select_fusion
  24.9 3.3 %fusion.3 = bf16[256,2048]{1,0:T(8,128)(2,1)S(1)} fusion(bf16[256,2048]{1,0:T(8,128)(2,1)S(1)} %maximum_select_fusion, s32[2048]{0:T(1024)S(1)} %copy-done.13), kind=kOutput, calls=%fused_computation.6 | convolution fusion | flops 2152202240 | bytes 2105344 | tf_op jit(solution)/shard_map/dot_general | solution.py:16
  28.3 2.4 convolution_convert_fusion.1
  30.7 1.3 collective-permute-start.2
  32.0 0.7 fusion.31
  33.1 0.6 collective-permute-done.3
  33.7 0.5 copy-done.9
  34.5 3.5 %fusion.17.back = f32[256,1024]{1,0:T(8,128)} fusion(bf16[1024,2048]{1,0:T(8,128)(2,1)S(1)} %copy-done.9, bf16[256,1024]{1,0:T(8,128)(2,1)} %collective-permute-done.3, bf16[256,1024]{1,0:T(8,128)(2,1)S(1)} %copy-done.10, pred[]{:T(512)S(6)} %eq.12), kind=kOutput, calls=%fused_computation.19 | convolution fusion | flops 1078460416 | bytes 6291457 | tf_op jit(solution)/shard_map/dot_general | solution.py:16
  38.0 0.6 fusion.32
  38.7 3.3 %collective-permute-start.1 = (bf16[16,1024]{1,0:T(8,128)(2,1)S(1)}, bf16[16,1024]{1,0:T(8,128)(2,1)S(1)}, u32[]{:S(2)}, u32[]{:S(2)}) collective-permute-start(bf16[16,1024]{1,0:T(8,128)(2,1)S(1)} %get-tuple-element.31), channel_id=1, source_target_pairs={{0,2},{2,4},{4,6},{6,8},{8,10},{10,12},{12,14},{14,16},{16,18},{18... | collective-permute-start | bytes 98312 | tf_op jit(solution)/shard_map/ppermute | solution.py:182
  42.1 0.6 collective-permute-done.1
  42.8 9.6 %shard_map.138 = (f32[256,1024]{1,0:T(8,128)S(1)}, f32[2,256,1024]{2,1,0:T(8,128)}, f32[2,256,1024]{2,1,0:T(8,128)}, bf16[4,16,1024]{2,1,0:T(8,128)(2,1)}, f32[1,1024]{1,0:T(1,128)S(1)}) custom-call(bf16[272,1024]{1,0:T(8,128)(2,1)S(1)} %pad_maximum_fusion.4.xf, bf16[272,1024]{1,0:T(8,128)(2,1)S(1)} %pad_maximum_fusion.5.xr, f32[256,1024]{1,0:T(8,128)S(1)} %copy-done, ...), custom_call_target="tpu_custom_call" | custom-call | tf_op jit(solution)/shard_map/pallas_call | solution.py:137
  52.5 24.4 %all-gather.2 = f32[16,2,16]{2,1,0:T(2,128)S(1)} all-gather(f32[1,2,16]{2,1,0:T(2,128)S(1)} %bitcast.37), channel_id=2, replica_groups=mesh['ctx'=16,'ch'=2] {'ctx'}, dimensions={0}, use_global_device_ids=true | all-gather | bytes 2176 | tf_op jit(solution)/shard_map/all_gather | solution.py:188
  77.4 0.9 mul.128
  78.3 19.4 %all-gather.8.cloned.1.call-done = bf16[64,16,1024]{2,1,0:T(8,128)(2,1)} async-done(((bf16[4,16,1024]{2,1,0:T(8,128)(2,1)}), bf16[64,16,1024]{2,1,0:T(8,128)(2,1)}) %all-gather.8.cloned.1.call-update) | async-done | bytes 2097168 | tf_op jit(solution)/shard_map/all_gather | solution.py:208
  97.7 2.2 fusion.2.carried
  99.9 5.7 %shard_map.139 = (bf16[256,1024]{1,0:T(8,128)(2,1)S(1)}, bf16[512,1024]{1,0:T(8,128)(2,1)S(1)}, f32[2,8,1024]{2,1,0:T(8,128)S(1)}, f32[2,8,1024]{2,1,0:T(8,128)S(1)}, f32[4,1024]{1,0:T(4,128)S(1)}) custom-call(bf16[272,1024]{1,0:T(8,128)(2,1)S(1)} %pad_maximum_fusion.4.xf, bf16[272,1024]{1,0:T(8,128)(2,1)S(1)} %pad_maximum_fusion.5.xr, ...), custom_call_target="tpu_custom_call" | custom-call | tf_op jit(solution)/shard_map/pallas_call | solution.py:137
  105.7 1.6 collective-permute-start.5
  107.3 3.0 %collective-permute-start.6 = (f32[8,1024]{1,0:T(8,128)S(1)}, f32[8,1024]{1,0:T(8,128)S(1)}, u32[]{:S(2)}, u32[]{:S(2)}) collective-permute-start(f32[8,1024]{1,0:T(8,128)S(1)} %get-tuple-element.39), channel_id=1, source_target_pairs={{0,2},{2,4},{4,6},{6,8},{8,10},{10,12},{12,14},{14,16},{16,18},{18... | collective-permute-start | bytes 98312 | tf_op jit(solution)/shard_map/ppermute | solution.py:239
  110.4 0.8 collective-permute-done.6
  111.2 4.4 %convolution_convert_fusion = bf16[2048,1024]{1,0:T(8,128)(2,1)} fusion(bf16[248,1024]{1,0:T(8,128)(2,1)S(1)} %get-tuple-element.27, bf16[8,1024]{1,0:T(8,128)(2,1)S(1)} %get-tuple-element.37, bf16[8,1024]{1,0:T(8,128)(2,1)S(1)} %get-tuple-element.36, bf16[248,1024]{1,0:T(8,128)(2,1)S(1)} %get-tuple-element.26, bf16[256,2048]{1,0:T(8,128)(2,1)S(1)} %copy-done.15, ...), kind=kOutput, calls=%fused_computation.5 | convolution fusion | flops 2157969408 | bytes 7340032 | tf_op jit(solution)/shard_map/dot_general | solution.py:16
  115.7 74.5 %reduce-scatter.2.cloned.1.call-done = bf16[128,1024]{1,0:T(8,128)(2,1)} async-done(((bf16[2048,1024]{1,0:T(8,128)(2,1)}), bf16[128,1024]{1,0:T(8,128)(2,1)}) %reduce-scatter.2.cloned.1.call-update) | async-done | bytes 262160 | tf_op jit(solution)/shard_map/reduce_scatter | solution.py:268
  190.3 2.3 fusion.14
  192.6 1.5 collective-permute-start.4
  194.1 58.7 %psum.7 = f32[5,1024]{1,0:T(8,128)S(1)} all-reduce(f32[5,1024]{1,0:T(8,128)S(1)} %pad_maximum_fusion.7), channel_id=1, replica_groups=mesh['ctx'=16,'ch'=2] {'ctx'}, use_global_device_ids=true, to_apply=%region_3.4 | all-reduce | flops 5120 | bytes 40960 | tf_op jit(solution)/shard_map/psum | solution.py:267
  252.8 0.6 slice.124
  253.4 0.6 slice.123
  254.0 3.1 %fusion.11 = bf16[256,1024]{1,0:T(8,128)(2,1)} fusion(bf16[256,1024]{1,0:T(8,128)(2,1)S(1)} %copy-done.4, bf16[1024,2048]{1,0:T(8,128)(2,1)} %param.20, s32[]{:T(128)S(6)} %select_n.68, bf16[256,1024]{1,0:T(8,128)(2,1)S(1)} %collective-permute-done.4), kind=kOutput, calls=%fused_computation.14 | convolution fusion | flops 537657344 | bytes 3670020 | tf_op jit(solution)/shard_map/dot_general | solution.py:16
  257.2 6.6 %convert_element_type.41 = f32[2048,1024]{1,0:T(8,128)} convert(bf16[2048,1024]{1,0:T(8,128)(2,1)} %all-gather.6.cloned.1.call-done) | non-fusion elementwise | flops 2097152 | bytes 12582912 | tf_op jit(solution)/shard_map/convert_element_type | solution.py:269
  (61 shorter events, 1.8 us)
Async XLA Ops:
  7.2 17.7 %copy-start.13 = (s32[2048]{0:T(1024)S(1)}, s32[2048]{0:T(1024)}, u32[]{:S(2)}) copy-start(s32[2048]{0:T(1024)} %param.12) | copy-start | bytes 24580
  7.2 90.5 %all-gather.8.cloned.1.call-start = ((), (), s32[]{:S(2)}) async-start(), calls=%async_computation.3 | async-start | bytes 2228224 | tf_op jit(solution)/shard_map/all_gather | solution.py:208
  7.2 16.0 %collective-permute-start = (bf16[256,1024]{1,0:T(8,128)(2,1)}, bf16[256,1024]{1,0:T(8,128)(2,1)S(1)}, u32[]{:S(2)}, u32[]{:S(2)}) collective-permute-start(bf16[256,1024]{1,0:T(8,128)(2,1)} %param.11), channel_id=1, source_target_pairs={{0,1},{1,0},{2,3},{3,2},{4,5},{5,4},{6,7},{7,6},{8,9},{9,8},{10,11... | collective-permute-start | bytes 1572872 | tf_op jit(solution)/shard_map/ppermute | solution.py:167
  10.3 23.5 %collective-permute-start.3 = (bf16[256,1024]{1,0:T(8,128)(2,1)}, bf16[256,1024]{1,0:T(8,128)(2,1)}, u32[]{:S(2)}, u32[]{:S(2)}) collective-permute-start(bf16[256,1024]{1,0:T(8,128)(2,1)} %param.21), channel_id=1, source_target_pairs={{0,1},{1,0},{2,3},{3,2},{4,5},{5,4},{6,7},{7,6},{8,9},{9,8},{10,11... | collective-permute-start | bytes 1572872 | tf_op jit(solution)/shard_map/ppermute | solution.py:167
  24.9 7.1 %copy-start.5 = (bf16[256,2048]{1,0:T(8,128)(2,1)}, bf16[256,2048]{1,0:T(8,128)(2,1)S(1)}, u32[]{:S(2)}) copy-start(bf16[256,2048]{1,0:T(8,128)(2,1)S(1)} %maximum_select_fusion) | copy-start | bytes 3145732
  24.9 3.4 %copy-start.8 = (bf16[2048,1024]{1,0:T(8,128)(2,1)S(1)}, bf16[2048,1024]{1,0:T(8,128)(2,1)}, u32[]{:S(2)}) copy-start(bf16[2048,1024]{1,0:T(8,128)(2,1)} %param.13) | copy-start | bytes 12582916
  28.2 3.7 %copy-start.14 = (bf16[256,2048]{1,0:T(8,128)(2,1)}, bf16[256,2048]{1,0:T(8,128)(2,1)S(1)}, u32[]{:S(2)}) copy-start(bf16[256,2048]{1,0:T(8,128)(2,1)S(1)} %fusion.3) | copy-start | bytes 3145732
  28.3 3.7 %copy-start.11 = (bf16[2048,32]{0,1:T(8,128)(2,1)S(1)}, bf16[2048,32]{0,1:T(8,128)(2,1)}, u32[]{:S(2)}) copy-start(bf16[2048,32]{0,1:T(8,128)(2,1)} %param.14) | copy-start | bytes 393220
  28.3 3.7 %copy-start.12 = (bf16[2048,16]{0,1:T(8,128)(2,1)S(1)}, bf16[2048,16]{0,1:T(8,128)(2,1)}, u32[]{:S(2)}) copy-start(bf16[2048,16]{0,1:T(8,128)(2,1)} %param.15) | copy-start | bytes 196612
  30.7 2.1 copy-start.7
  30.7 11.4 %collective-permute-start.2 = (bf16[16,1024]{1,0:T(8,128)(2,1)S(1)}, bf16[16,1024]{1,0:T(8,128)(2,1)S(1)}, u32[]{:S(2)}, u32[]{:S(2)}) collective-permute-start(bf16[16,1024]{1,0:T(8,128)(2,1)S(1)} %get-tuple-element.30), channel_id=1, source_target_pairs={{2,0},{4,2},{6,4},{8,6},{10,8},{12,10},{14,12},{16,14},{18,16},{20... | collective-permute-start | bytes 98312 | tf_op jit(solution)/shard_map/ppermute | solution.py:183
  32.0 2.2 copy-start.9
  32.7 1.8 copy-start.10
  38.0 4.8 %copy-start.1 = (f32[4,1024]{1,0:T(4,128)S(1)}, f32[4,1024]{1,0:T(4,128)}, u32[]{:S(2)}) copy-start(f32[4,1024]{1,0:T(4,128)} %taps.3) | copy-start | bytes 49156
  38.0 4.8 %copy-start.2 = (f32[1024]{0:T(1024)S(1)}, f32[1024]{0:T(1024)}, u32[]{:S(2)}) copy-start(f32[1024]{0:T(1024)} %param.19) | copy-start | bytes 12292
  38.7 4.1 %copy-start = (f32[256,1024]{1,0:T(8,128)S(1)}, f32[256,1024]{1,0:T(8,128)}, u32[]{:S(2)}) copy-start(f32[256,1024]{1,0:T(8,128)} %fusion.17.back) | copy-start | bytes 3145732
  38.7 4.0 %collective-permute-start.1 = (bf16[16,1024]{1,0:T(8,128)(2,1)S(1)}, bf16[16,1024]{1,0:T(8,128)(2,1)S(1)}, u32[]{:S(2)}, u32[]{:S(2)}) collective-permute-start(bf16[16,1024]{1,0:T(8,128)(2,1)S(1)} %get-tuple-element.31), channel_id=1, source_target_pairs={{0,2},{2,4},{4,6},{6,8},{8,10},{10,12},{12,14},{14,16},{16,18},{18... | collective-permute-start | bytes 98312 | tf_op jit(solution)/shard_map/ppermute | solution.py:182
  52.4 137.8 %reduce-scatter.2.cloned.1.call-start = ((), (), s32[]{:S(2)}) async-start(), calls=%async_computation.1 | async-start | bytes 4456448 | tf_op jit(solution)/shard_map/reduce_scatter | solution.py:268
  105.7 5.5 %copy-start.3 = (bf16[256,1024]{1,0:T(8,128)(2,1)}, bf16[256,1024]{1,0:T(8,128)(2,1)S(1)}, u32[]{:S(2)}) copy-start(bf16[256,1024]{1,0:T(8,128)(2,1)S(1)} %get-tuple-element.18) | copy-start | bytes 1572868
  105.7 5.5 %copy-start.6 = (bf16[256,2048]{1,0:T(8,128)(2,1)S(1)}, bf16[256,2048]{1,0:T(8,128)(2,1)}, u32[]{:S(2)}) copy-start(bf16[256,2048]{1,0:T(8,128)(2,1)} %copy-done.5) | copy-start | bytes 3145732
  105.7 5.5 %copy-start.15 = (bf16[256,2048]{1,0:T(8,128)(2,1)S(1)}, bf16[256,2048]{1,0:T(8,128)(2,1)}, u32[]{:S(2)}) copy-start(bf16[256,2048]{1,0:T(8,128)(2,1)} %copy-done.14) | copy-start | bytes 3145732
  105.7 4.7 %collective-permute-start.5 = (f32[8,1024]{1,0:T(8,128)S(1)}, f32[8,1024]{1,0:T(8,128)S(1)}, u32[]{:S(2)}, u32[]{:S(2)}) collective-permute-start(f32[8,1024]{1,0:T(8,128)S(1)} %get-tuple-element.38), channel_id=1, source_target_pairs={{2,0},{4,2},{6,4},{8,6},{10,8},{12,10},{14,12},{16,14},{18,16},{20... | collective-permute-start | bytes 98312 | tf_op jit(solution)/shard_map/ppermute | solution.py:238
  107.3 3.9 %collective-permute-start.6 = (f32[8,1024]{1,0:T(8,128)S(1)}, f32[8,1024]{1,0:T(8,128)S(1)}, u32[]{:S(2)}, u32[]{:S(2)}) collective-permute-start(f32[8,1024]{1,0:T(8,128)S(1)} %get-tuple-element.39), channel_id=1, source_target_pairs={{0,2},{2,4},{4,6},{6,8},{8,10},{10,12},{12,14},{14,16},{16,18},{18... | collective-permute-start | bytes 98312 | tf_op jit(solution)/shard_map/ppermute | solution.py:239
  115.6 74.6 %copy-start.4 = (bf16[256,1024]{1,0:T(8,128)(2,1)S(1)}, bf16[256,1024]{1,0:T(8,128)(2,1)}, u32[]{:S(2)}) copy-start(bf16[256,1024]{1,0:T(8,128)(2,1)} %copy-done.3) | copy-start | bytes 1572868
  115.7 141.5 %all-gather.6.cloned.1.call-start = ((), (), s32[]{:S(2)}) async-start(), calls=%async_computation.2 | async-start | bytes 4456448 | tf_op jit(solution)/shard_map/all_gather | solution.py:269
  192.6 61.4 %collective-permute-start.4 = (bf16[256,1024]{1,0:T(8,128)(2,1)S(1)}, bf16[256,1024]{1,0:T(8,128)(2,1)S(1)}, u32[]{:S(2)}, u32[]{:S(2)}) collective-permute-start(bf16[256,1024]{1,0:T(8,128)(2,1)S(1)} %fusion.14), channel_id=1, source_target_pairs={{0,1},{1,0},{2,3},{3,2},{4,5},{5,4},{6,7},{7,6},{8,9},{9,8},{10,11... | collective-permute-start | bytes 1572872 | tf_op jit(solution)/shard_map/ppermute | solution.py:244
Sparse Core Ops, SparseCore 0:
  52.5 45.1 all-gather.7
  115.8 74.3 reduce-scatter.1
  192.6 50.0 all-gather.5
where the time goes:
time: 271 us; the launch traced here: 270 us
  waiting for transfers between devices  108 us (40%)
  blocking collectives  83.1 us (31%)
  matrix products  20.5 us (8%)
  Pallas kernels  15.3 us (6%)
  between operations  14.2 us (5%)
  starting transfers between devices  14 us (5%)
  other arithmetic  11.7 us (4%)
  local copies, waits for them, and re-layouts  3.46 us (1%)
    reduce_scatter x1, waiting for transfers between devices, per_device(): lax.psum_scatter(weight_local, 'ctx', scatter_dimension=0, tiled=True)  74.5 us
    psum x1, blocking collectives, per_device(): tiny = lax.psum(jnp.concatenate([filt, skip], 0), 'ctx')  58.7 us
    all_gather x1, blocking collectives, per_device(): totals = lax.all_gather(jnp.sum(decays, axis=1), 'ctx')  24.4 us
    dot_general x7, matrix products, dot(): lax.dot_general(a, b, (dims, ((), ())), preferred_element_type=F32, preci...  19.8 us
    all_gather x1, waiting for transfers between devices, per_device(): pieces = lax.all_gather(ends, 'ctx')  19.4 us
    pallas_call x2, Pallas kernels, vmem_call(): pl.pallas_call(body, out_shape=[jax.ShapeDtypeStruct(*s) for s in shapes]...  15.3 us
    ppermute x2, waiting for transfers between devices, gathered(): other = lax.ppermute(part, 'ch', swap)  12.8 us
    convert_element_type x1, other arithmetic, per_device(): lax.all_gather(weight_sum, 'ctx', axis=0, tiled=True).astype(F32)  6.63 us
  transfers between devices with their start and end apart: 10, of which 6 were waited for; matrix products, arithmetic and copies ran while one was open for 8% of the time, Pallas kernels for 0%

commit v1 on v0

--- a/solution.py
+++ b/solution.py
@@ -132,6 +132,47 @@
             filt[k : k + 1, cols] = grads[k]
 
 
+def three_parts(value):
+    parts = []
+    for _ in range(3):
+        top = lax.reduce_precision(value, 8, 7)
+        parts.append(top.astype(BF16))
+        value = value - top
+    rows = jnp.concatenate(parts, 0)
+    return jnp.pad(rows, ((0, -rows.shape[0] % 16), (0, 0)))
+
+
+def summed_rows(value, axis):
+    count, me = lax.axis_size(axis), lax.axis_index(axis)
+    bits = [1 << b for b in range(count.bit_length() - 1)]
+    orders = (bits, bits[:1] + bits[2:] + bits[1:2])
+    half = value.shape[0] // 2
+    parts = [value[:half], value[half:]]
+
+    def swapped(part, bit):
+        return lax.ppermute(part, axis, [(i, i ^ bit) for i in range(count)])
+
+    for step in range(len(bits)):
+        for p in range(2):
+            bit = orders[p][step]
+            upper = (me // bit) % 2
+            rows = parts[p].shape[0] // 2
+            keep = lax.dynamic_slice_in_dim(parts[p], upper * rows, rows, 0)
+            send = lax.dynamic_slice_in_dim(parts[p], (1 - upper) * rows, rows, 0)
+            parts[p] = (keep.astype(F32) + swapped(send, bit).astype(F32)).astype(BF16)
+    for step in reversed(range(len(bits))):
+        for p in range(2):
+            bit = orders[p][step]
+            upper = (me // bit) % 2
+            other = swapped(parts[p], bit)
+            parts[p] = jnp.where(
+                upper == 0,
+                jnp.concatenate([parts[p], other], 0),
+                jnp.concatenate([other, parts[p]], 0),
+            )
+    return jnp.concatenate(parts, 0)
+
+
 def vmem_call(body, shapes, *operands):
     spec = pl.BlockSpec(memory_space=pltpu.VMEM)
     return pl.pallas_call(
@@ -185,7 +226,7 @@
     reads = small[:, :, states : 2 * states]
     sizes = jax.nn.softplus(small[:, :, 2 * states :] + step_bias[None, None, :])
     decays = -jnp.exp(decay_log)[None, None, :] * sizes
-    totals = lax.all_gather(jnp.sum(decays, axis=1), "ctx")
+    totals = three_parts(jnp.repeat(jnp.sum(decays, axis=1), depth, axis=1))
     lower = jnp.tril(jnp.ones((length, length), F32))
     sums = jnp.stack([lower, lower.T])
     run = jnp.einsum("bts,bsh->bth", sums, decays, precision=EXACT)
@@ -205,7 +246,12 @@
         ],
         xf, xr, back, sizes, run, run_t, writes, reads, filter_taps, skip_gain[None, :],
     )
-    pieces = lax.all_gather(ends, "ctx")
+    rows = 4 * states
+    packed = jnp.concatenate([ends.reshape(rows, width), totals], 0)
+    arrived = lax.all_gather(packed, "ctx")
+    pieces = arrived[:, :rows].reshape(count, 4, states, width)
+    totals = arrived[:, rows : rows + 6].astype(F32).reshape(count, 3, 2, heads, depth)
+    totals = jnp.sum(totals[..., 0], axis=1)
     j = jnp.arange(count)
     between = ((j[:, None] < j[None, :]) & (j[None, :] < me)) | (
         (j[None, :] < j[:, None]) & (j[None, :] > me)
@@ -265,8 +311,7 @@
     )
     weight_local = dot(both, grad_inner, ((0,), (0,))).astype(BF16)
     tiny = lax.psum(jnp.concatenate([filt, skip], 0), "ctx")
-    weight_sum = lax.psum_scatter(weight_local, "ctx", scatter_dimension=0, tiled=True)
-    weight_grad = lax.all_gather(weight_sum, "ctx", axis=0, tiled=True).astype(F32)
+    weight_grad = summed_rows(weight_local, "ctx").astype(F32)
     return (layer_out, weight_grad, tiny[:taken], tiny[taken])
 
 

time: 271 us -> 299 us (1.10)
  blocking collectives: 83.1 us -> 61.1 us
  waiting for transfers between devices: 108 us -> 124 us
  starting transfers between devices: 14 us -> 29.1 us
  other arithmetic: 11.7 us -> 23.4 us
  local copies, waits for them, and re-layouts: 3.46 us -> 8.78 us
    reduce_scatter x1 -> x0, waiting for transfers between devices: 74.5 us -> none  [per_device(): lax.psum_scatter(weight_local, 'ctx', scatter_dimension=0, tiled=True)]
    ppermute x0 -> x16, waiting for transfers between devices: none -> 63.3 us  [swapped(): return lax.ppermute(part, axis, [(i, i ^ bit) for i in range(count)])]
    all_gather x2 -> x1, waiting for transfers between devices: 19.4 us -> 47.1 us  [per_device(): arrived = lax.all_gather(packed, 'ctx')]
    all_gather x1 -> x0, blocking collectives: 24.4 us -> none  [per_device(): totals = lax.all_gather(jnp.sum(decays, axis=1), 'ctx')]
    ppermute x0 -> x16, starting transfers between devices: none -> 15.1 us  [swapped(): return lax.ppermute(part, axis, [(i, i ^ bit) for i in range(count)])]
    select_n x0 -> x8, other arithmetic: none -> 7.59 us  [summed_rows(): jnp.where(upper == 0, jnp.concatenate([parts[p], other], 0), jnp.concaten...]
    convert_element_type x1 -> x10, other arithmetic: 6.63 us -> 9.87 us  [the longest x8 5.35 us: summed_rows(): parts[p] = (keep.astype(F32) + swapped(send, bit).astype(F32)).astype(BF16)]
  transfers between devices with their start and end apart: 10 -> 24, of which waited for: 6 -> 15; matrix products, arithmetic and copies ran while one was open for 8% -> 12% of each run, Pallas kernels for 0% -> 0%
where the time goes in v1:
time: 299 us
  waiting for transfers between devices  124 us (41%)
  blocking collectives  61.1 us (20%)
  starting transfers between devices  29.1 us (10%)
  other arithmetic  23.4 us (8%)
  matrix products  22 us (7%)
  Pallas kernels  15.6 us (5%)
  between operations  14.7 us (5%)
  local copies, waits for them, and re-layouts  8.78 us (3%)
    ppermute x16, waiting for transfers between devices, swapped(): return lax.ppermute(part, axis, [(i, i ^ bit) for i in range(count)])  63.3 us
    psum x1, blocking collectives, per_device(): tiny = lax.psum(jnp.concatenate([filt, skip], 0), 'ctx')  61.1 us
    all_gather x1, waiting for transfers between devices, per_device(): arrived = lax.all_gather(packed, 'ctx')  47.1 us
    dot_general x7, matrix products, dot(): lax.dot_general(a, b, (dims, ((), ())), preferred_element_type=F32, preci...  21.3 us
    pallas_call x2, Pallas kernels, vmem_call(): pl.pallas_call(body, out_shape=[jax.ShapeDtypeStruct(*s) for s in shapes]...  15.6 us
    ppermute x16, starting transfers between devices, swapped(): return lax.ppermute(part, axis, [(i, i ^ bit) for i in range(count)])  15.1 us
    ppermute x2, waiting for transfers between devices, gathered(): other = lax.ppermute(part, 'ch', swap)  12.2 us
    select_n x8, other arithmetic, summed_rows(): jnp.where(upper == 0, jnp.concatenate([parts[p], other], 0), jnp.concaten...  7.59 us
  transfers between devices with their start and end apart: 24, of which 15 were waited for; matrix products, arithmetic and copies ran while one was open for 12% of the time, Pallas kernels for 0%

profile of v1, /device:TPU:0, one launch (start us, length us, event | category | flops | bytes accessed | tf_op | source)
XLA Modules:
  0.0 298.7 jit_solution(10410412213215643903)
XLA Ops:
  7.2 3.0 %collective-permute-start = (bf16[256,1024]{1,0:T(8,128)(2,1)}, bf16[256,1024]{1,0:T(8,128)(2,1)S(1)}, u32[]{:S(2)}, u32[]{:S(2)}) collective-permute-start(bf16[256,1024]{1,0:T(8,128)(2,1)} %param.11), channel_id=1, source_target_pairs={{0,1},{1,0},{2,3},{3,2},{4,5},{5,4},{6,7},{7,6},{8,9},{9,8},{10,11... | collective-permute-start | bytes 1572872 | tf_op jit(solution)/shard_map/ppermute | solution.py:208
  11.0 12.2 %collective-permute-done = bf16[256,1024]{1,0:T(8,128)(2,1)S(1)} collective-permute-done((bf16[256,1024]{1,0:T(8,128)(2,1)}, bf16[256,1024]{1,0:T(8,128)(2,1)S(1)}, u32[]{:S(2)}, u32[]{:S(2)}) %collective-permute-start) | collective-permute-done | bytes 524320 | tf_op jit(solution)/shard_map/ppermute | solution.py:208
  24.9 3.4 %fusion.3 = bf16[256,2048]{1,0:T(8,128)(2,1)S(1)} fusion(bf16[256,2048]{1,0:T(8,128)(2,1)S(1)} %maximum_select_fusion.2, s32[2048]{0:T(1024)S(1)} %copy-done.14), kind=kOutput, calls=%fused_computation.7 | convolution fusion | flops 2152202240 | bytes 2105344 | tf_op jit(solution)/shard_map/dot_general | solution.py:16
  29.7 5.0 %convolution_convert_fusion.1 = bf16[512,1024]{1,0:T(8,128)(2,1)S(1)} fusion(bf16[2048,1024]{1,0:T(8,128)(2,1)} %param.13, bf16[256,2048]{1,0:T(8,128)(2,1)} %copy-done.15, bf16[256,2048]{1,0:T(8,128)(2,1)S(1)} %maximum_select_fusion.2), kind=kOutput, calls=%fused_computation.17 | convolution fusion | flops 2152202240 | bytes 7340032 | tf_op jit(solution)/shard_map/dot_general | solution.py:16
  36.9 3.6 %fusion.17.back = f32[256,1024]{1,0:T(8,128)} fusion(bf16[1024,2048]{1,0:T(8,128)(2,1)S(1)} %copy-done.10, bf16[256,1024]{1,0:T(8,128)(2,1)} %collective-permute-done.3, bf16[256,1024]{1,0:T(8,128)(2,1)S(1)} %copy-done.11, pred[]{:T(512)S(6)} %eq.45), kind=kOutput, calls=%fused_computation.24 | convolution fusion | flops 1078460416 | bytes 6291457 | tf_op jit(solution)/shard_map/dot_general | solution.py:16
  40.7 3.3 %collective-permute-start.1 = (bf16[16,1024]{1,0:T(8,128)(2,1)S(1)}, bf16[16,1024]{1,0:T(8,128)(2,1)S(1)}, u32[]{:S(2)}, u32[]{:S(2)}) collective-permute-start(bf16[16,1024]{1,0:T(8,128)(2,1)S(1)} %get-tuple-element.33), channel_id=1, source_target_pairs={{0,2},{2,4},{4,6},{6,8},{8,10},{10,12},{12,14},{14,16},{16,18},{18... | collective-permute-start | bytes 98312 | tf_op jit(solution)/shard_map/ppermute | solution.py:223
  44.8 9.7 %shard_map.138 = (f32[256,1024]{1,0:T(8,128)S(1)}, f32[2,256,1024]{2,1,0:T(8,128)}, f32[2,256,1024]{2,1,0:T(8,128)}, bf16[4,16,1024]{2,1,0:T(8,128)(2,1)S(1)}, f32[1,1024]{1,0:T(1,128)S(1)}) custom-call(bf16[272,1024]{1,0:T(8,128)(2,1)S(1)} %pad_maximum_fusion.4.xf, bf16[272,1024]{1,0:T(8,128)(2,1)S(1)} %pad_maximum_fusion.5.xr, f32[256,1024]{1,0:T(8,128)S(1)} %copy-done, ...), custom_call_target="tpu_custom_call" | custom-call | tf_op jit(solution)/shard_map/pallas_call | solution.py:178
  55.2 47.1 %all-gather.3.cloned.1.call-done = bf16[1280,1024]{1,0:T(8,128)(2,1)} async-done(((bf16[80,1024]{1,0:T(8,128)(2,1)}), bf16[1280,1024]{1,0:T(8,128)(2,1)}) %all-gather.3.cloned.1.call-update) | async-done | bytes 2621456 | tf_op jit(solution)/shard_map/all_gather | solution.py:251
  106.8 2.2 fusion.2
  109.0 6.0 %shard_map.139 = (bf16[256,1024]{1,0:T(8,128)(2,1)S(1)}, bf16[512,1024]{1,0:T(8,128)(2,1)S(1)}, f32[2,8,1024]{2,1,0:T(8,128)S(1)}, f32[2,8,1024]{2,1,0:T(8,128)S(1)}, f32[4,1024]{1,0:T(4,128)S(1)}) custom-call(bf16[272,1024]{1,0:T(8,128)(2,1)S(1)} %pad_maximum_fusion.4.xf, bf16[272,1024]{1,0:T(8,128)(2,1)S(1)} %pad_maximum_fusion.5.xr, ...), custom_call_target="tpu_custom_call" | custom-call | tf_op jit(solution)/shard_map/pallas_call | solution.py:178
  116.6 3.0 %collective-permute-start.6 = (f32[8,1024]{1,0:T(8,128)S(1)}, f32[8,1024]{1,0:T(8,128)S(1)}, u32[]{:S(2)}, u32[]{:S(2)}) collective-permute-start(f32[8,1024]{1,0:T(8,128)S(1)} %get-tuple-element.41), channel_id=1, source_target_pairs={{0,2},{2,4},{4,6},{6,8},{8,10},{10,12},{12,14},{14,16},{16,18},{18... | collective-permute-start | bytes 98312 | tf_op jit(solution)/shard_map/ppermute | solution.py:285
  120.5 2.4 convolution_convert_fusion
  126.7 2.1 collective-permute-done.15
  128.8 1.9 add_convert_fusion
  131.7 3.5 %collective-permute-start.16 = (bf16[256,1024]{1,0:T(8,128)(2,1)}, bf16[256,1024]{1,0:T(8,128)(2,1)}, u32[]{:S(2)}, u32[]{:S(2)}) collective-permute-start(bf16[256,1024]{1,0:T(8,128)(2,1)} %constant_dynamic-slice_fusion.2), channel_id=1, source_target_pairs={{0,8},{2,10},{4,12},{6,14},{8,0},{10,2},{12,4},{14,6},{16,24},{18,... | collective-permute-start | bytes 1572872 | tf_op jit(solution)/shard_map/ppermute | solution.py:153
  137.3 10.4 %collective-permute-done.16 = bf16[256,1024]{1,0:T(8,128)(2,1)} collective-permute-done((bf16[256,1024]{1,0:T(8,128)(2,1)}, bf16[256,1024]{1,0:T(8,128)(2,1)}, u32[]{:S(2)}, u32[]{:S(2)}) %collective-permute-start.16) | collective-permute-done | bytes 524320 | tf_op jit(solution)/shard_map/ppermute | solution.py:153
  149.1 2.5 collective-permute-start.17
  152.7 10.9 %collective-permute-done.17 = bf16[128,1024]{1,0:T(8,128)(2,1)S(1)} collective-permute-done((bf16[128,1024]{1,0:T(8,128)(2,1)S(1)}, bf16[128,1024]{1,0:T(8,128)(2,1)S(1)}, u32[]{:S(2)}, u32[]{:S(2)}) %collective-permute-start.17) | collective-permute-done | bytes 262176 | tf_op jit(solution)/shard_map/ppermute | solution.py:153
  165.2 3.6 %collective-permute-done.18 = bf16[64,1024]{1,0:T(8,128)(2,1)S(1)} collective-permute-done((bf16[64,1024]{1,0:T(8,128)(2,1)S(1)}, bf16[64,1024]{1,0:T(8,128)(2,1)S(1)}, u32[]{:S(2)}, u32[]{:S(2)}) %collective-permute-start.18) | collective-permute-done | bytes 131104 | tf_op jit(solution)/shard_map/ppermute | solution.py:153
  169.3 2.9 collective-permute-done.10
  175.3 9.9 %collective-permute-done.11 = bf16[64,1024]{1,0:T(8,128)(2,1)S(1)} collective-permute-done((bf16[64,1024]{1,0:T(8,128)(2,1)S(1)}, bf16[64,1024]{1,0:T(8,128)(2,1)S(1)}, u32[]{:S(2)}, u32[]{:S(2)}) %collective-permute-start.11) | collective-permute-done | bytes 131104 | tf_op jit(solution)/shard_map/ppermute | solution.py:153
  185.4 5.1 %collective-permute-done.20 = bf16[128,1024]{1,0:T(8,128)(2,1)S(1)} collective-permute-done((bf16[128,1024]{1,0:T(8,128)(2,1)S(1)}, bf16[128,1024]{1,0:T(8,128)(2,1)S(1)}, u32[]{:S(2)}, u32[]{:S(2)}) %collective-permute-start.20) | collective-permute-done | bytes 262176 | tf_op jit(solution)/shard_map/ppermute | solution.py:153
  190.7 5.4 %collective-permute-done.12 = bf16[128,1024]{1,0:T(8,128)(2,1)S(1)} collective-permute-done((bf16[128,1024]{1,0:T(8,128)(2,1)S(1)}, bf16[128,1024]{1,0:T(8,128)(2,1)S(1)}, u32[]{:S(2)}, u32[]{:S(2)}) %collective-permute-start.12) | collective-permute-done | bytes 262176 | tf_op jit(solution)/shard_map/ppermute | solution.py:153
  196.3 2.0 collective-permute-start.13
  198.2 9.0 %collective-permute-done.21 = bf16[256,1024]{1,0:T(8,128)(2,1)S(1)} collective-permute-done((bf16[256,1024]{1,0:T(8,128)(2,1)S(1)}, bf16[256,1024]{1,0:T(8,128)(2,1)S(1)}, u32[]{:S(2)}, u32[]{:S(2)}) %collective-permute-start.21) | collective-permute-done | bytes 524320 | tf_op jit(solution)/shard_map/ppermute | solution.py:153
  207.9 2.4 collective-permute-done.13
  212.1 3.1 %fusion.14 = bf16[256,1024]{1,0:T(8,128)(2,1)} fusion(bf16[256,1024]{1,0:T(8,128)(2,1)S(1)} %copy-done.4, bf16[1024,2048]{1,0:T(8,128)(2,1)} %param.20, s32[]{:T(128)S(6)} %select_n.233), kind=kOutput, calls=%fused_computation.20 | convolution fusion | flops 537133056 | bytes 3145732 | tf_op jit(solution)/shard_map/dot_general | solution.py:16
  216.7 61.1 %psum.7 = f32[5,1024]{1,0:T(8,128)S(1)} all-reduce(f32[5,1024]{1,0:T(8,128)S(1)} %pad_maximum_fusion.8), channel_id=1, replica_groups=mesh['ctx'=16,'ch'=2] {'ctx'}, use_global_device_ids=true, to_apply=%region_3.4 | all-reduce | flops 5120 | bytes 40960 | tf_op jit(solution)/shard_map/psum | solution.py:313
  279.0 3.1 %fusion.11 = bf16[256,1024]{1,0:T(8,128)(2,1)} fusion(bf16[256,1024]{1,0:T(8,128)(2,1)S(1)} %copy-done.4, bf16[1024,2048]{1,0:T(8,128)(2,1)} %param.20, s32[]{:T(128)S(6)} %select_n.232, bf16[256,1024]{1,0:T(8,128)(2,1)S(1)} %collective-permute-done.4), kind=kOutput, calls=%fused_computation.19 | convolution fusion | flops 537657344 | bytes 3670020 | tf_op jit(solution)/shard_map/dot_general | solution.py:16
  282.2 2.6 maximum_select_fusion.1
  284.8 2.6 maximum_select_fusion
  287.3 4.5 %maximum_convert_fusion = f32[2048,1024]{1,0:T(8,128)} fusion(bf16[1024,1024]{1,0:T(8,128)(2,1)S(1)} %maximum_select_fusion.1, bf16[1024,1024]{1,0:T(8,128)(2,1)S(1)} %maximum_select_fusion), kind=kLoop, calls=%fused_computation.3 | loop fusion | flops 8388608 | bytes 12582912 | tf_op jit(solution)/shard_map/convert_element_type | solution.py:314
  (122 shorter events, 34.4 us)
Async XLA Ops:
  7.2 17.7 %copy-start.14 = (s32[2048]{0:T(1024)S(1)}, s32[2048]{0:T(1024)}, u32[]{:S(2)}) copy-start(s32[2048]{0:T(1024)} %param.12) | copy-start | bytes 24580
  7.2 95.1 %all-gather.3.cloned.1.call-start = ((), (), s32[]{:S(2)}) async-start(), calls=%async_computation | async-start | bytes 2785280 | tf_op jit(solution)/shard_map/all_gather | solution.py:251
  7.2 16.0 %collective-permute-start = (bf16[256,1024]{1,0:T(8,128)(2,1)}, bf16[256,1024]{1,0:T(8,128)(2,1)S(1)}, u32[]{:S(2)}, u32[]{:S(2)}) collective-permute-start(bf16[256,1024]{1,0:T(8,128)(2,1)} %param.11), channel_id=1, source_target_pairs={{0,1},{1,0},{2,3},{3,2},{4,5},{5,4},{6,7},{7,6},{8,9},{9,8},{10,11... | collective-permute-start | bytes 1572872 | tf_op jit(solution)/shard_map/ppermute | solution.py:208
  10.3 26.7 %collective-permute-start.3 = (bf16[256,1024]{1,0:T(8,128)(2,1)}, bf16[256,1024]{1,0:T(8,128)(2,1)}, u32[]{:S(2)}, u32[]{:S(2)}) collective-permute-start(bf16[256,1024]{1,0:T(8,128)(2,1)} %param.21), channel_id=1, source_target_pairs={{0,1},{1,0},{2,3},{3,2},{4,5},{5,4},{6,7},{7,6},{8,9},{9,8},{10,11... | collective-permute-start | bytes 1572872 | tf_op jit(solution)/shard_map/ppermute | solution.py:208
  24.9 4.9 %copy-start.7 = (bf16[256,2048]{1,0:T(8,128)(2,1)}, bf16[256,2048]{1,0:T(8,128)(2,1)S(1)}, u32[]{:S(2)}) copy-start(bf16[256,2048]{1,0:T(8,128)(2,1)S(1)} %maximum_select_fusion.2) | copy-start | bytes 3145732
  29.7 7.2 %copy-start.10 = (bf16[1024,2048]{1,0:T(8,128)(2,1)S(1)}, bf16[1024,2048]{1,0:T(8,128)(2,1)}, u32[]{:S(2)}) copy-start(bf16[1024,2048]{1,0:T(8,128)(2,1)} %param.20) | copy-start | bytes 12582916
  34.8 9.2 %collective-permute-start.2 = (bf16[16,1024]{1,0:T(8,128)(2,1)S(1)}, bf16[16,1024]{1,0:T(8,128)(2,1)S(1)}, u32[]{:S(2)}, u32[]{:S(2)}) collective-permute-start(bf16[16,1024]{1,0:T(8,128)(2,1)S(1)} %get-tuple-element.32), channel_id=1, source_target_pairs={{2,0},{4,2},{6,4},{8,6},{10,8},{12,10},{14,12},{16,14},{18,16},{20... | collective-permute-start | bytes 98312 | tf_op jit(solution)/shard_map/ppermute | solution.py:224
  40.7 4.0 %collective-permute-start.1 = (bf16[16,1024]{1,0:T(8,128)(2,1)S(1)}, bf16[16,1024]{1,0:T(8,128)(2,1)S(1)}, u32[]{:S(2)}, u32[]{:S(2)}) collective-permute-start(bf16[16,1024]{1,0:T(8,128)(2,1)S(1)} %get-tuple-element.33), channel_id=1, source_target_pairs={{0,2},{2,4},{4,6},{6,8},{8,10},{10,12},{12,14},{14,16},{16,18},{18... | collective-permute-start | bytes 98312 | tf_op jit(solution)/shard_map/ppermute | solution.py:223
  115.0 8.0 %copy-start.3 = (bf16[256,1024]{1,0:T(8,128)(2,1)}, bf16[256,1024]{1,0:T(8,128)(2,1)S(1)}, u32[]{:S(2)}) copy-start(bf16[256,1024]{1,0:T(8,128)(2,1)S(1)} %get-tuple-element.18) | copy-start | bytes 1572868
  115.0 5.5 %copy-start.8 = (bf16[256,2048]{1,0:T(8,128)(2,1)S(1)}, bf16[256,2048]{1,0:T(8,128)(2,1)}, u32[]{:S(2)}) copy-start(bf16[256,2048]{1,0:T(8,128)(2,1)} %copy-done.7) | copy-start | bytes 3145732
  115.0 5.5 %copy-start.16 = (bf16[256,2048]{1,0:T(8,128)(2,1)S(1)}, bf16[256,2048]{1,0:T(8,128)(2,1)}, u32[]{:S(2)}) copy-start(bf16[256,2048]{1,0:T(8,128)(2,1)} %copy-done.15) | copy-start | bytes 3145732
  115.0 4.7 %collective-permute-start.5 = (f32[8,1024]{1,0:T(8,128)S(1)}, f32[8,1024]{1,0:T(8,128)S(1)}, u32[]{:S(2)}, u32[]{:S(2)}) collective-permute-start(f32[8,1024]{1,0:T(8,128)S(1)} %get-tuple-element.40), channel_id=1, source_target_pairs={{2,0},{4,2},{6,4},{8,6},{10,8},{12,10},{14,12},{16,14},{18,16},{20... | collective-permute-start | bytes 98312 | tf_op jit(solution)/shard_map/ppermute | solution.py:284
  116.6 3.9 %collective-permute-start.6 = (f32[8,1024]{1,0:T(8,128)S(1)}, f32[8,1024]{1,0:T(8,128)S(1)}, u32[]{:S(2)}, u32[]{:S(2)}) collective-permute-start(f32[8,1024]{1,0:T(8,128)S(1)} %get-tuple-element.41), channel_id=1, source_target_pairs={{0,2},{2,4},{4,6},{6,8},{8,10},{10,12},{12,14},{14,16},{16,18},{18... | collective-permute-start | bytes 98312 | tf_op jit(solution)/shard_map/ppermute | solution.py:285
  124.5 4.3 %collective-permute-start.15 = (bf16[512,1024]{1,0:T(8,128)(2,1)}, bf16[512,1024]{1,0:T(8,128)(2,1)}, u32[]{:S(2)}, u32[]{:S(2)}) collective-permute-start(bf16[512,1024]{1,0:T(8,128)(2,1)} %constant_dynamic-slice_fusion.3), channel_id=1, source_target_pairs={{0,2},{2,0},{4,6},{6,4},{8,10},{10,8},{12,14},{14,12},{16,18},{18,... | collective-permute-start | bytes 3145736 | tf_op jit(solution)/shard_map/ppermute | solution.py:153
  126.3 8.9 %collective-permute-start.7 = (bf16[512,1024]{1,0:T(8,128)(2,1)S(1)}, bf16[512,1024]{1,0:T(8,128)(2,1)}, u32[]{:S(2)}, u32[]{:S(2)}) collective-permute-start(bf16[512,1024]{1,0:T(8,128)(2,1)S(1)} %constant_dynamic-slice_fusion.7), channel_id=1, source_target_pairs={{0,2},{2,0},{4,6},{6,4},{8,10},{10,8},{12,14},{14,12},{16,18},{18,... | collective-permute-start | bytes 3145736 | tf_op jit(solution)/shard_map/ppermute | solution.py:153
  130.8 6.0 %copy-start.6 = (bf16[512,1024]{1,0:T(8,128)(2,1)}, bf16[512,1024]{1,0:T(8,128)(2,1)S(1)}, u32[]{:S(2)}) copy-start(bf16[512,1024]{1,0:T(8,128)(2,1)S(1)} %add_convert_fusion) | copy-start | bytes 3145732
  131.7 16.0 %collective-permute-start.16 = (bf16[256,1024]{1,0:T(8,128)(2,1)}, bf16[256,1024]{1,0:T(8,128)(2,1)}, u32[]{:S(2)}, u32[]{:S(2)}) collective-permute-start(bf16[256,1024]{1,0:T(8,128)(2,1)} %constant_dynamic-slice_fusion.2), channel_id=1, source_target_pairs={{0,8},{2,10},{4,12},{6,14},{8,0},{10,2},{12,4},{14,6},{16,24},{18,... | collective-permute-start | bytes 1572872 | tf_op jit(solution)/shard_map/ppermute | solution.py:153
  136.8 14.8 %collective-permute-start.8 = (bf16[256,1024]{1,0:T(8,128)(2,1)S(1)}, bf16[256,1024]{1,0:T(8,128)(2,1)S(1)}, u32[]{:S(2)}, u32[]{:S(2)}) collective-permute-start(bf16[256,1024]{1,0:T(8,128)(2,1)S(1)} %constant_dynamic-slice_fusion.6), channel_id=1, source_target_pairs={{0,4},{2,6},{4,0},{6,2},{8,12},{10,14},{12,8},{14,10},{16,20},{18,... | collective-permute-start | bytes 1572872 | tf_op jit(solution)/shard_map/ppermute | solution.py:153
  149.1 14.5 %collective-permute-start.17 = (bf16[128,1024]{1,0:T(8,128)(2,1)S(1)}, bf16[128,1024]{1,0:T(8,128)(2,1)S(1)}, u32[]{:S(2)}, u32[]{:S(2)}) collective-permute-start(bf16[128,1024]{1,0:T(8,128)(2,1)S(1)} %constant_dynamic-slice_fusion.1), channel_id=1, source_target_pairs={{0,16},{2,18},{4,20},{6,22},{8,24},{10,26},{12,28},{14,30},{16,0},... | collective-permute-start | bytes 786440 | tf_op jit(solution)/shard_map/ppermute | solution.py:153
  151.9 12.3 %collective-permute-start.9 = (bf16[128,1024]{1,0:T(8,128)(2,1)S(1)}, bf16[128,1024]{1,0:T(8,128)(2,1)S(1)}, u32[]{:S(2)}, u32[]{:S(2)}) collective-permute-start(bf16[128,1024]{1,0:T(8,128)(2,1)S(1)} %constant_dynamic-slice_fusion.5), channel_id=1, source_target_pairs={{0,8},{2,10},{4,12},{6,14},{8,0},{10,2},{12,4},{14,6},{16,24},{18,... | collective-permute-start | bytes 786440 | tf_op jit(solution)/shard_map/ppermute | solution.py:153
  163.7 5.0 %collective-permute-start.18 = (bf16[64,1024]{1,0:T(8,128)(2,1)S(1)}, bf16[64,1024]{1,0:T(8,128)(2,1)S(1)}, u32[]{:S(2)}, u32[]{:S(2)}) collective-permute-start(bf16[64,1024]{1,0:T(8,128)(2,1)S(1)} %constant_dynamic-slice_fusion), channel_id=1, source_target_pairs={{0,4},{2,6},{4,0},{6,2},{8,12},{10,14},{12,8},{14,10},{16,20},{18,... | collective-permute-start | bytes 393224 | tf_op jit(solution)/shard_map/ppermute | solution.py:153
  164.3 7.9 %collective-permute-start.10 = (bf16[64,1024]{1,0:T(8,128)(2,1)S(1)}, bf16[64,1024]{1,0:T(8,128)(2,1)S(1)}, u32[]{:S(2)}, u32[]{:S(2)}) collective-permute-start(bf16[64,1024]{1,0:T(8,128)(2,1)S(1)} %constant_dynamic-slice_fusion.4), channel_id=1, source_target_pairs={{0,16},{2,18},{4,20},{6,22},{8,24},{10,26},{12,28},{14,30},{16,0},... | collective-permute-start | bytes 393224 | tf_op jit(solution)/shard_map/ppermute | solution.py:153
  168.8 5.0 %collective-permute-start.19 = (bf16[64,1024]{1,0:T(8,128)(2,1)S(1)}, bf16[64,1024]{1,0:T(8,128)(2,1)S(1)}, u32[]{:S(2)}, u32[]{:S(2)}) collective-permute-start(bf16[64,1024]{1,0:T(8,128)(2,1)S(1)} %add_convert_fusion.6), channel_id=1, source_target_pairs={{0,4},{2,6},{4,0},{6,2},{8,12},{10,14},{12,8},{14,10},{16,20},{18,... | collective-permute-start | bytes 393224 | tf_op jit(solution)/shard_map/ppermute | solution.py:153
  172.2 13.0 %collective-permute-start.11 = (bf16[64,1024]{1,0:T(8,128)(2,1)S(1)}, bf16[64,1024]{1,0:T(8,128)(2,1)S(1)}, u32[]{:S(2)}, u32[]{:S(2)}) collective-permute-start(bf16[64,1024]{1,0:T(8,128)(2,1)S(1)} %add_convert_fusion.7), channel_id=1, source_target_pairs={{0,16},{2,18},{4,20},{6,22},{8,24},{10,26},{12,28},{14,30},{16,0},... | collective-permute-start | bytes 393224 | tf_op jit(solution)/shard_map/ppermute | solution.py:153
  173.9 16.6 %collective-permute-start.20 = (bf16[128,1024]{1,0:T(8,128)(2,1)S(1)}, bf16[128,1024]{1,0:T(8,128)(2,1)S(1)}, u32[]{:S(2)}, u32[]{:S(2)}) collective-permute-start(bf16[128,1024]{1,0:T(8,128)(2,1)S(1)} %maximum_select_fusion.10), channel_id=1, source_target_pairs={{0,16},{2,18},{4,20},{6,22},{8,24},{10,26},{12,28},{14,30},{16,0},... | collective-permute-start | bytes 786440 | tf_op jit(solution)/shard_map/ppermute | solution.py:153
  185.3 10.8 %collective-permute-start.12 = (bf16[128,1024]{1,0:T(8,128)(2,1)S(1)}, bf16[128,1024]{1,0:T(8,128)(2,1)S(1)}, u32[]{:S(2)}, u32[]{:S(2)}) collective-permute-start(bf16[128,1024]{1,0:T(8,128)(2,1)S(1)} %maximum_select_fusion.9), channel_id=1, source_target_pairs={{0,8},{2,10},{4,12},{6,14},{8,0},{10,2},{12,4},{14,6},{16,24},{18,... | collective-permute-start | bytes 786440 | tf_op jit(solution)/shard_map/ppermute | solution.py:153
  190.7 16.6 %collective-permute-start.21 = (bf16[256,1024]{1,0:T(8,128)(2,1)S(1)}, bf16[256,1024]{1,0:T(8,128)(2,1)S(1)}, u32[]{:S(2)}, u32[]{:S(2)}) collective-permute-start(bf16[256,1024]{1,0:T(8,128)(2,1)S(1)} %maximum_select_fusion.8), channel_id=1, source_target_pairs={{0,8},{2,10},{4,12},{6,14},{8,0},{10,2},{12,4},{14,6},{16,24},{18,... | collective-permute-start | bytes 1572872 | tf_op jit(solution)/shard_map/ppermute | solution.py:153
  196.3 14.1 %collective-permute-start.13 = (bf16[256,1024]{1,0:T(8,128)(2,1)S(1)}, bf16[256,1024]{1,0:T(8,128)(2,1)}, u32[]{:S(2)}, u32[]{:S(2)}) collective-permute-start(bf16[256,1024]{1,0:T(8,128)(2,1)S(1)} %maximum_select_fusion.7), channel_id=1, source_target_pairs={{0,4},{2,6},{4,0},{6,2},{8,12},{10,14},{12,8},{14,10},{16,20},{18,... | collective-permute-start | bytes 1572872 | tf_op jit(solution)/shard_map/ppermute | solution.py:153
  198.2 13.8 %copy-start.4 = (bf16[256,1024]{1,0:T(8,128)(2,1)S(1)}, bf16[256,1024]{1,0:T(8,128)(2,1)}, u32[]{:S(2)}) copy-start(bf16[256,1024]{1,0:T(8,128)(2,1)} %copy-done.3) | copy-start | bytes 1572868
  207.7 74.4 %collective-permute-start.22 = (bf16[512,1024]{1,0:T(8,128)(2,1)S(1)}, bf16[512,1024]{1,0:T(8,128)(2,1)}, u32[]{:S(2)}, u32[]{:S(2)}) collective-permute-start(bf16[512,1024]{1,0:T(8,128)(2,1)S(1)} %maximum_select_fusion.6), channel_id=1, source_target_pairs={{0,2},{2,0},{4,6},{6,4},{8,10},{10,8},{12,14},{14,12},{16,18},{18,... | collective-permute-start | bytes 3145736 | tf_op jit(solution)/shard_map/ppermute | solution.py:153
  212.0 72.8 %collective-permute-start.14 = (bf16[512,1024]{1,0:T(8,128)(2,1)S(1)}, bf16[512,1024]{1,0:T(8,128)(2,1)}, u32[]{:S(2)}, u32[]{:S(2)}) collective-permute-start(bf16[512,1024]{1,0:T(8,128)(2,1)S(1)} %maximum_select_fusion.5), channel_id=1, source_target_pairs={{0,2},{2,0},{4,6},{6,4},{8,10},{10,8},{12,14},{14,12},{16,18},{18,... | collective-permute-start | bytes 3145736 | tf_op jit(solution)/shard_map/ppermute | solution.py:153
  215.2 63.8 %collective-permute-start.4 = (bf16[256,1024]{1,0:T(8,128)(2,1)}, bf16[256,1024]{1,0:T(8,128)(2,1)S(1)}, u32[]{:S(2)}, u32[]{:S(2)}) collective-permute-start(bf16[256,1024]{1,0:T(8,128)(2,1)} %fusion.14), channel_id=1, source_target_pairs={{0,1},{1,0},{2,3},{3,2},{4,5},{5,4},{6,7},{7,6},{8,9},{9,8},{10,11... | collective-permute-start | bytes 1572872 | tf_op jit(solution)/shard_map/ppermute | solution.py:290
  (9 other events, 26.4 us)
Sparse Core Ops, SparseCore 0:
  55.3 46.9 all-gather.2

commit v2 on v1

--- a/solution.py
+++ b/solution.py
@@ -142,6 +142,41 @@
     return jnp.pad(rows, ((0, -rows.shape[0] % 16), (0, 0)))
 
 
+def summed_whole(value, axis):
+    count = lax.axis_size(axis)
+    for b in range(count.bit_length() - 1):
+        value = value + lax.ppermute(value, axis, [(i, i ^ (1 << b)) for i in range(count)])
+    return value
+
+
+def entering(ends, totals, axis):
+    count, me = lax.axis_size(axis), lax.axis_index(axis)
+    kinds, states, width = ends.shape
+    rows = kinds * states
+    group = ends.astype(F32)
+    result = jnp.zeros_like(group)
+    passed = jnp.zeros((kinds, width), F32)
+    forward = jnp.array([True, False, False, True])
+    for b in range(count.bit_length() - 1):
+        bit = 1 << b
+        packed = jnp.concatenate(
+            [group.astype(BF16).reshape(rows, width), three_parts(totals)], 0
+        )
+        arrived = lax.ppermute(packed, axis, [(i, i ^ bit) for i in range(count)]).astype(F32)
+        other = arrived[:rows].reshape(kinds, states, width)
+        added = sum(arrived[rows + 2 * k : rows + 2 * k + 2] for k in range(3))
+        source = (forward == ((me // bit) % 2 == 1))[:, None]
+        theirs, ours = jnp.tile(added, (2, 1)), jnp.tile(totals, (2, 1))
+        result = result + jnp.where(source, jnp.exp(passed), 0.0)[:, None] * other
+        passed = passed + jnp.where(source, theirs, 0.0)
+        group = (
+            jnp.where(source, jnp.exp(ours), 1.0)[:, None] * other
+            + jnp.where(source, 1.0, jnp.exp(theirs))[:, None] * group
+        )
+        totals = totals + added
+    return result
+
+
 def summed_rows(value, axis):
     count, me = lax.axis_size(axis), lax.axis_index(axis)
     bits = [1 << b for b in range(count.bit_length() - 1)]
@@ -226,7 +261,7 @@
     reads = small[:, :, states : 2 * states]
     sizes = jax.nn.softplus(small[:, :, 2 * states :] + step_bias[None, None, :])
     decays = -jnp.exp(decay_log)[None, None, :] * sizes
-    totals = three_parts(jnp.repeat(jnp.sum(decays, axis=1), depth, axis=1))
+    totals = jnp.repeat(jnp.sum(decays, axis=1), depth, axis=1)
     lower = jnp.tril(jnp.ones((length, length), F32))
     sums = jnp.stack([lower, lower.T])
     run = jnp.einsum("bts,bsh->bth", sums, decays, precision=EXACT)
@@ -246,30 +281,7 @@
         ],
         xf, xr, back, sizes, run, run_t, writes, reads, filter_taps, skip_gain[None, :],
     )
-    rows = 4 * states
-    packed = jnp.concatenate([ends.reshape(rows, width), totals], 0)
-    arrived = lax.all_gather(packed, "ctx")
-    pieces = arrived[:, :rows].reshape(count, 4, states, width)
-    totals = arrived[:, rows : rows + 6].astype(F32).reshape(count, 3, 2, heads, depth)
-    totals = jnp.sum(totals[..., 0], axis=1)
-    j = jnp.arange(count)
-    between = ((j[:, None] < j[None, :]) & (j[None, :] < me)) | (
-        (j[None, :] < j[:, None]) & (j[None, :] > me)
-    )
-    weight = jnp.exp(jnp.einsum("ji,ibh->jbh", between.astype(F32), totals, precision=EXACT))
-    earlier = jnp.where((j < me)[:, None], 1.0, 0.0)
-    later = jnp.where((j > me)[:, None], 1.0, 0.0)
-    kinds = jnp.stack(
-        [
-            weight[:, 0] * earlier,
-            weight[:, 1] * later,
-            weight[:, 0] * later,
-            weight[:, 1] * earlier,
-        ],
-        axis=1,
-    )
-    kinds = jnp.repeat(kinds, depth, axis=2)
-    carried = jnp.sum(kinds[:, :, None, :] * pieces.astype(F32), axis=0)
+    carried = entering(ends, totals, "ctx")
     mixed16, partial_grad, edge, slope_edge, filt = vmem_call(
         functools.partial(carry_kernel, depth, group),
         [
@@ -310,7 +322,7 @@
         0,
     )
     weight_local = dot(both, grad_inner, ((0,), (0,))).astype(BF16)
-    tiny = lax.psum(jnp.concatenate([filt, skip], 0), "ctx")
+    tiny = summed_whole(jnp.concatenate([filt, skip], 0), "ctx")
     weight_grad = summed_rows(weight_local, "ctx").astype(F32)
     return (layer_out, weight_grad, tiny[:taken], tiny[taken])
 

time: 299 us -> 223 us (0.75)
  blocking collectives: 61.1 us -> 0 us
  waiting for transfers between devices: 124 us -> 83.8 us
  starting transfers between devices: 29.1 us -> 52.7 us
  between operations: 14.7 us -> 1.54 us
  other arithmetic: 23.4 us -> 31.5 us
  local copies, waits for them, and re-layouts: 8.78 us -> 15 us
    psum x1 -> x0, blocking collectives: 61.1 us -> none  [per_device(): tiny = lax.psum(jnp.concatenate([filt, skip], 0), 'ctx')]
    all_gather x1 -> x0, waiting for transfers between devices: 47.1 us -> none  [per_device(): arrived = lax.all_gather(packed, 'ctx')]
    ppermute x0 -> x8, waiting for transfers between devices: none -> 20.4 us  [the longest x4 10.2 us: entering(): lax.ppermute(packed, axis, [(i, i ^ bit) for i in range(count)]).astype(F32)]
    ppermute x0 -> x8, starting transfers between devices: none -> 16.6 us  [the longest x4 9.99 us: entering(): lax.ppermute(packed, axis, [(i, i ^ bit) for i in range(count)]).astype(F32)]
    ppermute x16, waiting for transfers between devices: 63.3 us -> 49.8 us  [swapped(): return lax.ppermute(part, axis, [(i, i ^ bit) for i in range(count)])]
    ppermute x16, starting transfers between devices: 15.1 us -> 22.2 us  [swapped(): return lax.ppermute(part, axis, [(i, i ^ bit) for i in range(count)])]
    another operation x1 -> x9, local copies, waits for them, and re-layouts: 0.02 us -> 5.83 us  [entering(): theirs, ours = (jnp.tile(added, (2, 1)), jnp.tile(totals, (2, 1)))]
  transfers between devices with their start and end apart: 24 -> 31, of which waited for: 15 -> 23; matrix products, arithmetic and copies ran while one was open for 12% -> 19% of each run, Pallas kernels for 0% -> 0%
where the time goes in v2:
time: 223 us; the launch traced here: 222 us
  waiting for transfers between devices  83.8 us (38%)
  starting transfers between devices  52.7 us (24%)
  other arithmetic  31.5 us (14%)
  matrix products  21.9 us (10%)
  Pallas kernels  15.5 us (7%)
  local copies, waits for them, and re-layouts  15 us (7%)
    ppermute x16, waiting for transfers between devices, swapped(): return lax.ppermute(part, axis, [(i, i ^ bit) for i in range(count)])  49.8 us
    ppermute x16, starting transfers between devices, swapped(): return lax.ppermute(part, axis, [(i, i ^ bit) for i in range(count)])  22.2 us
    dot_general x7, matrix products, dot(): lax.dot_general(a, b, (dims, ((), ())), preferred_element_type=F32, preci...  21.3 us
    pallas_call x2, Pallas kernels, vmem_call(): pl.pallas_call(body, out_shape=[jax.ShapeDtypeStruct(*s) for s in shapes]...  15.5 us
    ppermute x2, waiting for transfers between devices, gathered(): other = lax.ppermute(part, 'ch', swap)  12.2 us
    ppermute x4, waiting for transfers between devices, entering(): lax.ppermute(packed, axis, [(i, i ^ bit) for i in range(count)]).astype(F32)  10.2 us
    ppermute x4, waiting for transfers between devices, summed_whole(): lax.ppermute(value, axis, [(i, i ^ 1 << b) for i in range(count)])  10.2 us
    ppermute x4, starting transfers between devices, entering(): lax.ppermute(packed, axis, [(i, i ^ bit) for i in range(count)]).astype(F32)  9.99 us
  transfers between devices with their start and end apart: 31, of which 23 were waited for; matrix products, arithmetic and copies ran while one was open for 19% of the time, Pallas kernels for 0%

profile of v2, /device:TPU:0, one launch (start us, length us, event | category | flops | bytes accessed | tf_op | source)
XLA Modules:
  0.0 221.8 jit_solution(15102217640953682756)
XLA Ops:
  0.6 3.0 %collective-permute-start = (bf16[256,1024]{1,0:T(8,128)(2,1)}, bf16[256,1024]{1,0:T(8,128)(2,1)S(1)}, u32[]{:S(2)}, u32[]{:S(2)}) collective-permute-start(bf16[256,1024]{1,0:T(8,128)(2,1)} %param.12), channel_id=1, source_target_pairs={{0,1},{1,0},{2,3},{3,2},{4,5},{5,4},{6,7},{7,6},{8,9},{9,8},{10,11... | collective-permute-start | bytes 1572872 | tf_op jit(solution)/shard_map/ppermute | solution.py:243
  4.5 12.2 %collective-permute-done = bf16[256,1024]{1,0:T(8,128)(2,1)S(1)} collective-permute-done((bf16[256,1024]{1,0:T(8,128)(2,1)}, bf16[256,1024]{1,0:T(8,128)(2,1)S(1)}, u32[]{:S(2)}, u32[]{:S(2)}) %collective-permute-start) | collective-permute-done | bytes 524320 | tf_op jit(solution)/shard_map/ppermute | solution.py:243
  18.3 3.4 %fusion.2 = bf16[256,2048]{1,0:T(8,128)(2,1)S(1)} fusion(bf16[256,2048]{1,0:T(8,128)(2,1)S(1)} %maximum_select_fusion.2, s32[2048]{0:T(1024)S(1)} %copy-done.27), kind=kOutput, calls=%fused_computation.5 | convolution fusion | flops 2152202240 | bytes 2105344 | tf_op jit(solution)/shard_map/dot_general | solution.py:16
  23.2 5.0 %convolution_convert_fusion.1 = bf16[512,1024]{1,0:T(8,128)(2,1)S(1)} fusion(bf16[2048,1024]{1,0:T(8,128)(2,1)} %param.14, bf16[256,2048]{1,0:T(8,128)(2,1)} %copy-done.28, bf16[256,2048]{1,0:T(8,128)(2,1)S(1)} %maximum_select_fusion.2), kind=kOutput, calls=%fused_computation.15 | convolution fusion | flops 2152202240 | bytes 7340032 | tf_op jit(solution)/shard_map/dot_general | solution.py:16
  30.4 3.6 %fusion.16.back = f32[256,1024]{1,0:T(8,128)} fusion(bf16[1024,2048]{1,0:T(8,128)(2,1)S(1)} %copy-done.23, bf16[256,1024]{1,0:T(8,128)(2,1)} %collective-permute-done.3, bf16[256,1024]{1,0:T(8,128)(2,1)S(1)} %copy-done.24, pred[]{:T(512)S(6)} %eq.85), kind=kOutput, calls=%fused_computation.21 | convolution fusion | flops 1078460416 | bytes 6291457 | tf_op jit(solution)/shard_map/dot_general | solution.py:16
  34.2 3.3 %collective-permute-start.1 = (bf16[16,1024]{1,0:T(8,128)(2,1)S(1)}, bf16[16,1024]{1,0:T(8,128)(2,1)S(1)}, u32[]{:S(2)}, u32[]{:S(2)}) collective-permute-start(bf16[16,1024]{1,0:T(8,128)(2,1)S(1)} %get-tuple-element.41), channel_id=1, source_target_pairs={{0,2},{2,4},{4,6},{6,8},{8,10},{10,12},{12,14},{14,16},{16,18},{18... | collective-permute-start | bytes 98312 | tf_op jit(solution)/shard_map/ppermute | solution.py:258
  38.2 9.5 %shard_map.147 = (f32[256,1024]{1,0:T(8,128)S(1)}, f32[2,256,1024]{2,1,0:T(8,128)}, f32[2,256,1024]{2,1,0:T(8,128)}, bf16[4,16,1024]{2,1,0:T(8,128)(2,1)S(1)}, f32[1,1024]{1,0:T(1,128)S(1)}) custom-call(bf16[272,1024]{1,0:T(8,128)(2,1)S(1)} %pad_maximum_fusion.4.xf, bf16[272,1024]{1,0:T(8,128)(2,1)S(1)} %pad_maximum_fusion.5.xr, f32[256,1024]{1,0:T(8,128)S(1)} %copy-done, ...), custom_call_target="tpu_custom_call" | custom-call | tf_op jit(solution)/shard_map/pallas_call | solution.py:213
  57.2 2.8 %collective-permute-done.5 = bf16[80,1024]{1,0:T(8,128)(2,1)S(1)} collective-permute-done((bf16[80,1024]{1,0:T(8,128)(2,1)}, bf16[80,1024]{1,0:T(8,128)(2,1)S(1)}, u32[]{:S(2)}, u32[]{:S(2)}) %collective-permute-start.5) | collective-permute-done | bytes 163872 | tf_op jit(solution)/shard_map/ppermute | solution.py:165
  67.7 2.7 %collective-permute-start.6 = (bf16[80,1024]{1,0:T(8,128)(2,1)}, bf16[80,1024]{1,0:T(8,128)(2,1)S(1)}, u32[]{:S(2)}, u32[]{:S(2)}) collective-permute-start(bf16[80,1024]{1,0:T(8,128)(2,1)} %pad_maximum_fusion.8), channel_id=1, source_target_pairs={{0,8},{2,10},{4,12},{6,14},{8,0},{10,2},{12,4},{14,6},{16,24},{18,... | collective-permute-start | bytes 491528 | tf_op jit(solution)/shard_map/ppermute | solution.py:165
  80.3 2.8 %collective-permute-start.7 = (bf16[80,1024]{1,0:T(8,128)(2,1)S(1)}, bf16[80,1024]{1,0:T(8,128)(2,1)S(1)}, u32[]{:S(2)}, u32[]{:S(2)}) collective-permute-start(bf16[80,1024]{1,0:T(8,128)(2,1)S(1)} %pad_maximum_fusion.9), channel_id=1, source_target_pairs={{0,16},{2,18},{4,20},{6,22},{8,24},{10,26},{12,28},{14,30},{16,0},... | collective-permute-start | bytes 491528 | tf_op jit(solution)/shard_map/ppermute | solution.py:165
  83.1 6.4 %collective-permute-done.7 = bf16[80,1024]{1,0:T(8,128)(2,1)S(1)} collective-permute-done((bf16[80,1024]{1,0:T(8,128)(2,1)S(1)}, bf16[80,1024]{1,0:T(8,128)(2,1)S(1)}, u32[]{:S(2)}, u32[]{:S(2)}) %collective-permute-start.7) | collective-permute-done | bytes 163872 | tf_op jit(solution)/shard_map/ppermute | solution.py:165
  89.8 6.0 %shard_map.148 = (bf16[256,1024]{1,0:T(8,128)(2,1)S(1)}, bf16[512,1024]{1,0:T(8,128)(2,1)S(1)}, f32[2,8,1024]{2,1,0:T(8,128)S(1)}, f32[2,8,1024]{2,1,0:T(8,128)S(1)}, f32[4,1024]{1,0:T(4,128)S(1)}) custom-call(bf16[272,1024]{1,0:T(8,128)(2,1)S(1)} %pad_maximum_fusion.4.xf, bf16[272,1024]{1,0:T(8,128)(2,1)S(1)} %pad_maximum_fusion.5.xr, ...), custom_call_target="tpu_custom_call" | custom-call | tf_op jit(solution)/shard_map/pallas_call | solution.py:213
  97.2 3.0 %collective-permute-start.10 = (f32[8,1024]{1,0:T(8,128)S(1)}, f32[8,1024]{1,0:T(8,128)S(1)}, u32[]{:S(2)}, u32[]{:S(2)}) collective-permute-start(f32[8,1024]{1,0:T(8,128)S(1)} %get-tuple-element.49), channel_id=1, source_target_pairs={{0,2},{2,4},{4,6},{6,8},{8,10},{10,12},{12,14},{14,16},{16,18},{18... | collective-permute-start | bytes 98312 | tf_op jit(solution)/shard_map/ppermute | solution.py:297
  109.9 3.3 %collective-permute-start.20 = (bf16[256,1024]{1,0:T(8,128)(2,1)}, bf16[256,1024]{1,0:T(8,128)(2,1)}, u32[]{:S(2)}, u32[]{:S(2)}) collective-permute-start(bf16[256,1024]{1,0:T(8,128)(2,1)} %constant_dynamic-slice_fusion.2), channel_id=1, source_target_pairs={{0,8},{2,10},{4,12},{6,14},{8,0},{10,2},{12,4},{14,6},{16,24},{18,... | collective-permute-start | bytes 1572872 | tf_op jit(solution)/shard_map/ppermute | solution.py:188
  115.1 10.7 %collective-permute-done.20 = bf16[256,1024]{1,0:T(8,128)(2,1)} collective-permute-done((bf16[256,1024]{1,0:T(8,128)(2,1)}, bf16[256,1024]{1,0:T(8,128)(2,1)}, u32[]{:S(2)}, u32[]{:S(2)}) %collective-permute-start.20) | collective-permute-done | bytes 524320 | tf_op jit(solution)/shard_map/ppermute | solution.py:188
  127.2 3.4 %collective-permute-start.21 = (bf16[128,1024]{1,0:T(8,128)(2,1)S(1)}, bf16[128,1024]{1,0:T(8,128)(2,1)S(1)}, u32[]{:S(2)}, u32[]{:S(2)}) collective-permute-start(bf16[128,1024]{1,0:T(8,128)(2,1)S(1)} %constant_dynamic-slice_fusion.1), channel_id=1, source_target_pairs={{0,16},{2,18},{4,20},{6,22},{8,24},{10,26},{12,28},{14,30},{16,0},... | collective-permute-start | bytes 786440 | tf_op jit(solution)/shard_map/ppermute | solution.py:188
  132.7 9.8 %collective-permute-done.21 = bf16[128,1024]{1,0:T(8,128)(2,1)S(1)} collective-permute-done((bf16[128,1024]{1,0:T(8,128)(2,1)S(1)}, bf16[128,1024]{1,0:T(8,128)(2,1)S(1)}, u32[]{:S(2)}, u32[]{:S(2)}) %collective-permute-start.21) | collective-permute-done | bytes 262176 | tf_op jit(solution)/shard_map/ppermute | solution.py:188
  144.0 3.6 %collective-permute-done.22 = bf16[64,1024]{1,0:T(8,128)(2,1)S(1)} collective-permute-done((bf16[64,1024]{1,0:T(8,128)(2,1)S(1)}, bf16[64,1024]{1,0:T(8,128)(2,1)S(1)}, u32[]{:S(2)}, u32[]{:S(2)}) %collective-permute-start.22) | collective-permute-done | bytes 131104 | tf_op jit(solution)/shard_map/ppermute | solution.py:188
  147.8 4.5 %collective-permute-done.14 = bf16[64,1024]{1,0:T(8,128)(2,1)S(1)} collective-permute-done((bf16[64,1024]{1,0:T(8,128)(2,1)S(1)}, bf16[64,1024]{1,0:T(8,128)(2,1)S(1)}, u32[]{:S(2)}, u32[]{:S(2)}) %collective-permute-start.14) | collective-permute-done | bytes 131104 | tf_op jit(solution)/shard_map/ppermute | solution.py:188
  152.8 2.7 %collective-permute-start.24 = (bf16[128,1024]{1,0:T(8,128)(2,1)S(1)}, bf16[128,1024]{1,0:T(8,128)(2,1)S(1)}, u32[]{:S(2)}, u32[]{:S(2)}) collective-permute-start(bf16[128,1024]{1,0:T(8,128)(2,1)S(1)} %maximum_select_fusion.10), channel_id=1, source_target_pairs={{0,16},{2,18},{4,20},{6,22},{8,24},{10,26},{12,28},{14,30},{16,0},... | collective-permute-start | bytes 786440 | tf_op jit(solution)/shard_map/ppermute | solution.py:188
  155.4 2.8 %collective-permute-done.15 = bf16[64,1024]{1,0:T(8,128)(2,1)S(1)} collective-permute-done((bf16[64,1024]{1,0:T(8,128)(2,1)S(1)}, bf16[64,1024]{1,0:T(8,128)(2,1)S(1)}, u32[]{:S(2)}, u32[]{:S(2)}) %collective-permute-start.15) | collective-permute-done | bytes 131104 | tf_op jit(solution)/shard_map/ppermute | solution.py:188
  158.3 5.8 %collective-permute-start.16 = (bf16[128,1024]{1,0:T(8,128)(2,1)S(1)}, bf16[128,1024]{1,0:T(8,128)(2,1)S(1)}, u32[]{:S(2)}, u32[]{:S(2)}) collective-permute-start(bf16[128,1024]{1,0:T(8,128)(2,1)S(1)} %maximum_select_fusion.9), channel_id=1, source_target_pairs={{0,8},{2,10},{4,12},{6,14},{8,0},{10,2},{12,4},{14,6},{16,24},{18,... | collective-permute-start | bytes 786440 | tf_op jit(solution)/shard_map/ppermute | solution.py:188
  164.1 5.4 %collective-permute-done.24 = bf16[128,1024]{1,0:T(8,128)(2,1)S(1)} collective-permute-done((bf16[128,1024]{1,0:T(8,128)(2,1)S(1)}, bf16[128,1024]{1,0:T(8,128)(2,1)S(1)}, u32[]{:S(2)}, u32[]{:S(2)}) %collective-permute-start.24) | collective-permute-done | bytes 262176 | tf_op jit(solution)/shard_map/ppermute | solution.py:188
  169.8 3.0 %collective-permute-done.16 = bf16[128,1024]{1,0:T(8,128)(2,1)S(1)} collective-permute-done((bf16[128,1024]{1,0:T(8,128)(2,1)S(1)}, bf16[128,1024]{1,0:T(8,128)(2,1)S(1)}, u32[]{:S(2)}, u32[]{:S(2)}) %collective-permute-start.16) | collective-permute-done | bytes 262176 | tf_op jit(solution)/shard_map/ppermute | solution.py:188
  172.9 2.9 %collective-permute-start.17 = (bf16[256,1024]{1,0:T(8,128)(2,1)S(1)}, bf16[256,1024]{1,0:T(8,128)(2,1)}, u32[]{:S(2)}, u32[]{:S(2)}) collective-permute-start(bf16[256,1024]{1,0:T(8,128)(2,1)S(1)} %maximum_select_fusion.7), channel_id=1, source_target_pairs={{0,4},{2,6},{4,0},{6,2},{8,12},{10,14},{12,8},{14,10},{16,20},{18,... | collective-permute-start | bytes 1572872 | tf_op jit(solution)/shard_map/ppermute | solution.py:188
  175.9 7.0 %collective-permute-done.25 = bf16[256,1024]{1,0:T(8,128)(2,1)S(1)} collective-permute-done((bf16[256,1024]{1,0:T(8,128)(2,1)S(1)}, bf16[256,1024]{1,0:T(8,128)(2,1)S(1)}, u32[]{:S(2)}, u32[]{:S(2)}) %collective-permute-start.25) | collective-permute-done | bytes 524320 | tf_op jit(solution)/shard_map/ppermute | solution.py:188
  186.3 3.1 %fusion.13 = bf16[256,1024]{1,0:T(8,128)(2,1)} fusion(bf16[256,1024]{1,0:T(8,128)(2,1)S(1)} %copy-done.4, bf16[1024,2048]{1,0:T(8,128)(2,1)} %param.21, s32[]{:T(128)S(6)} %select_n.345), kind=kOutput, calls=%fused_computation.18 | convolution fusion | flops 537133056 | bytes 3145732 | tf_op jit(solution)/shard_map/dot_general | solution.py:16
  192.9 3.4 %collective-permute-done.28 = f32[5,1024]{1,0:T(8,128)S(1)} collective-permute-done((f32[5,1024]{1,0:T(8,128)S(1)}, f32[5,1024]{1,0:T(8,128)S(1)}, u32[]{:S(2)}, u32[]{:S(2)}) %collective-permute-start.28) | collective-permute-done | bytes 20512 | tf_op jit(solution)/shard_map/ppermute | solution.py:148
  196.2 3.9 %collective-permute-done.29 = f32[5,1024]{1,0:T(8,128)S(1)} collective-permute-done((f32[5,1024]{1,0:T(8,128)S(1)}, f32[5,1024]{1,0:T(8,128)S(1)}, u32[]{:S(2)}, u32[]{:S(2)}) %collective-permute-start.29) | collective-permute-done | bytes 20512 | tf_op jit(solution)/shard_map/ppermute | solution.py:148
  200.2 5.7 %collective-permute-start.30 = (f32[5,1024]{1,0:T(8,128)S(1)}, f32[5,1024]{1,0:T(8,128)S(1)}, u32[]{:S(2)}, u32[]{:S(2)}) collective-permute-start(f32[5,1024]{1,0:T(8,128)S(1)} %add.291), channel_id=1, source_target_pairs={{0,16},{2,18},{4,20},{6,22},{8,24},{10,26},{12,28},{14,30},{16,0},... | collective-permute-start | bytes 61448 | tf_op jit(solution)/shard_map/ppermute | solution.py:148
  209.0 3.1 %fusion.10 = bf16[256,1024]{1,0:T(8,128)(2,1)} fusion(bf16[256,1024]{1,0:T(8,128)(2,1)S(1)} %copy-done.4, bf16[1024,2048]{1,0:T(8,128)(2,1)} %param.21, s32[]{:T(128)S(6)} %select_n.344, bf16[256,1024]{1,0:T(8,128)(2,1)S(1)} %collective-permute-done.8), kind=kOutput, calls=%fused_computation.17 | convolution fusion | flops 537657344 | bytes 3670020 | tf_op jit(solution)/shard_map/dot_general | solution.py:16
  217.3 4.5 %maximum_convert_fusion = f32[2048,1024]{1,0:T(8,128)} fusion(bf16[1024,1024]{1,0:T(8,128)(2,1)S(1)} %maximum_select_fusion.1, bf16[1024,1024]{1,0:T(8,128)(2,1)S(1)} %maximum_select_fusion), kind=kLoop, calls=%fused_computation.3 | loop fusion | flops 8388608 | bytes 12582912 | tf_op jit(solution)/shard_map/convert_element_type | solution.py:326
  (191 shorter events, 67.7 us)
Async XLA Ops:
  0.6 17.7 %copy-start.27 = (s32[2048]{0:T(1024)S(1)}, s32[2048]{0:T(1024)}, u32[]{:S(2)}) copy-start(s32[2048]{0:T(1024)} %param.13) | copy-start | bytes 24580
  0.6 16.0 %collective-permute-start = (bf16[256,1024]{1,0:T(8,128)(2,1)}, bf16[256,1024]{1,0:T(8,128)(2,1)S(1)}, u32[]{:S(2)}, u32[]{:S(2)}) collective-permute-start(bf16[256,1024]{1,0:T(8,128)(2,1)} %param.12), channel_id=1, source_target_pairs={{0,1},{1,0},{2,3},{3,2},{4,5},{5,4},{6,7},{7,6},{8,9},{9,8},{10,11... | collective-permute-start | bytes 1572872 | tf_op jit(solution)/shard_map/ppermute | solution.py:243
  3.7 26.7 %collective-permute-start.3 = (bf16[256,1024]{1,0:T(8,128)(2,1)}, bf16[256,1024]{1,0:T(8,128)(2,1)}, u32[]{:S(2)}, u32[]{:S(2)}) collective-permute-start(bf16[256,1024]{1,0:T(8,128)(2,1)} %param.22), channel_id=1, source_target_pairs={{0,1},{1,0},{2,3},{3,2},{4,5},{5,4},{6,7},{7,6},{8,9},{9,8},{10,11... | collective-permute-start | bytes 1572872 | tf_op jit(solution)/shard_map/ppermute | solution.py:243
  28.3 9.2 %collective-permute-start.2 = (bf16[16,1024]{1,0:T(8,128)(2,1)S(1)}, bf16[16,1024]{1,0:T(8,128)(2,1)S(1)}, u32[]{:S(2)}, u32[]{:S(2)}) collective-permute-start(bf16[16,1024]{1,0:T(8,128)(2,1)S(1)} %get-tuple-element.40), channel_id=1, source_target_pairs={{2,0},{4,2},{6,4},{8,6},{10,8},{12,10},{14,12},{16,14},{18,16},{20... | collective-permute-start | bytes 98312 | tf_op jit(solution)/shard_map/ppermute | solution.py:259
  34.2 4.0 %collective-permute-start.1 = (bf16[16,1024]{1,0:T(8,128)(2,1)S(1)}, bf16[16,1024]{1,0:T(8,128)(2,1)S(1)}, u32[]{:S(2)}, u32[]{:S(2)}) collective-permute-start(bf16[16,1024]{1,0:T(8,128)(2,1)S(1)} %get-tuple-element.41), channel_id=1, source_target_pairs={{0,2},{2,4},{4,6},{6,8},{8,10},{10,12},{12,14},{14,16},{16,18},{18... | collective-permute-start | bytes 98312 | tf_op jit(solution)/shard_map/ppermute | solution.py:258
  47.8 2.9 %collective-permute-start.4 = (bf16[80,1024]{1,0:T(8,128)(2,1)S(1)}, bf16[80,1024]{1,0:T(8,128)(2,1)S(1)}, u32[]{:S(2)}, u32[]{:S(2)}) collective-permute-start(bf16[80,1024]{1,0:T(8,128)(2,1)S(1)} %pad_maximum_fusion.6), channel_id=1, source_target_pairs={{0,2},{2,0},{4,6},{6,4},{8,10},{10,8},{12,14},{14,12},{16,18},{18,... | collective-permute-start | bytes 491528 | tf_op jit(solution)/shard_map/ppermute | solution.py:165
  52.7 7.3 %collective-permute-start.5 = (bf16[80,1024]{1,0:T(8,128)(2,1)}, bf16[80,1024]{1,0:T(8,128)(2,1)S(1)}, u32[]{:S(2)}, u32[]{:S(2)}) collective-permute-start(bf16[80,1024]{1,0:T(8,128)(2,1)} %pad_maximum_fusion.7), channel_id=1, source_target_pairs={{0,4},{2,6},{4,0},{6,2},{8,12},{10,14},{12,8},{14,10},{16,20},{18,... | collective-permute-start | bytes 491528 | tf_op jit(solution)/shard_map/ppermute | solution.py:165
  67.7 6.6 %collective-permute-start.6 = (bf16[80,1024]{1,0:T(8,128)(2,1)}, bf16[80,1024]{1,0:T(8,128)(2,1)S(1)}, u32[]{:S(2)}, u32[]{:S(2)}) collective-permute-start(bf16[80,1024]{1,0:T(8,128)(2,1)} %pad_maximum_fusion.8), channel_id=1, source_target_pairs={{0,8},{2,10},{4,12},{6,14},{8,0},{10,2},{12,4},{14,6},{16,24},{18,... | collective-permute-start | bytes 491528 | tf_op jit(solution)/shard_map/ppermute | solution.py:165
  80.3 9.3 %collective-permute-start.7 = (bf16[80,1024]{1,0:T(8,128)(2,1)S(1)}, bf16[80,1024]{1,0:T(8,128)(2,1)S(1)}, u32[]{:S(2)}, u32[]{:S(2)}) collective-permute-start(bf16[80,1024]{1,0:T(8,128)(2,1)S(1)} %pad_maximum_fusion.9), channel_id=1, source_target_pairs={{0,16},{2,18},{4,20},{6,22},{8,24},{10,26},{12,28},{14,30},{16,0},... | collective-permute-start | bytes 491528 | tf_op jit(solution)/shard_map/ppermute | solution.py:165
  95.8 4.5 %collective-permute-start.9 = (f32[8,1024]{1,0:T(8,128)S(1)}, f32[8,1024]{1,0:T(8,128)S(1)}, u32[]{:S(2)}, u32[]{:S(2)}) collective-permute-start(f32[8,1024]{1,0:T(8,128)S(1)} %get-tuple-element.48), channel_id=1, source_target_pairs={{2,0},{4,2},{6,4},{8,6},{10,8},{12,10},{14,12},{16,14},{18,16},{20... | collective-permute-start | bytes 98312 | tf_op jit(solution)/shard_map/ppermute | solution.py:296
  97.2 3.9 %collective-permute-start.10 = (f32[8,1024]{1,0:T(8,128)S(1)}, f32[8,1024]{1,0:T(8,128)S(1)}, u32[]{:S(2)}, u32[]{:S(2)}) collective-permute-start(f32[8,1024]{1,0:T(8,128)S(1)} %get-tuple-element.49), channel_id=1, source_target_pairs={{0,2},{2,4},{4,6},{6,8},{8,10},{10,12},{12,14},{14,16},{16,18},{18... | collective-permute-start | bytes 98312 | tf_op jit(solution)/shard_map/ppermute | solution.py:297
  104.1 3.0 %collective-permute-start.19 = (bf16[512,1024]{1,0:T(8,128)(2,1)S(1)}, bf16[512,1024]{1,0:T(8,128)(2,1)}, u32[]{:S(2)}, u32[]{:S(2)}) collective-permute-start(bf16[512,1024]{1,0:T(8,128)(2,1)S(1)} %constant_dynamic-slice_fusion.3), channel_id=1, source_target_pairs={{0,2},{2,0},{4,6},{6,4},{8,10},{10,8},{12,14},{14,12},{16,18},{18,... | collective-permute-start | bytes 3145736 | tf_op jit(solution)/shard_map/ppermute | solution.py:188
  105.7 7.5 %collective-permute-start.11 = (bf16[512,1024]{1,0:T(8,128)(2,1)}, bf16[512,1024]{1,0:T(8,128)(2,1)}, u32[]{:S(2)}, u32[]{:S(2)}) collective-permute-start(bf16[512,1024]{1,0:T(8,128)(2,1)} %constant_dynamic-slice_fusion.7), channel_id=1, source_target_pairs={{0,2},{2,0},{4,6},{6,4},{8,10},{10,8},{12,14},{14,12},{16,18},{18,... | collective-permute-start | bytes 3145736 | tf_op jit(solution)/shard_map/ppermute | solution.py:188
  109.9 15.9 %collective-permute-start.20 = (bf16[256,1024]{1,0:T(8,128)(2,1)}, bf16[256,1024]{1,0:T(8,128)(2,1)}, u32[]{:S(2)}, u32[]{:S(2)}) collective-permute-start(bf16[256,1024]{1,0:T(8,128)(2,1)} %constant_dynamic-slice_fusion.2), channel_id=1, source_target_pairs={{0,8},{2,10},{4,12},{6,14},{8,0},{10,2},{12,4},{14,6},{16,24},{18,... | collective-permute-start | bytes 1572872 | tf_op jit(solution)/shard_map/ppermute | solution.py:188
  115.0 15.7 %collective-permute-start.12 = (bf16[256,1024]{1,0:T(8,128)(2,1)S(1)}, bf16[256,1024]{1,0:T(8,128)(2,1)S(1)}, u32[]{:S(2)}, u32[]{:S(2)}) collective-permute-start(bf16[256,1024]{1,0:T(8,128)(2,1)S(1)} %constant_dynamic-slice_fusion.6), channel_id=1, source_target_pairs={{0,4},{2,6},{4,0},{6,2},{8,12},{10,14},{12,8},{14,10},{16,20},{18,... | collective-permute-start | bytes 1572872 | tf_op jit(solution)/shard_map/ppermute | solution.py:188
  127.2 15.3 %collective-permute-start.21 = (bf16[128,1024]{1,0:T(8,128)(2,1)S(1)}, bf16[128,1024]{1,0:T(8,128)(2,1)S(1)}, u32[]{:S(2)}, u32[]{:S(2)}) collective-permute-start(bf16[128,1024]{1,0:T(8,128)(2,1)S(1)} %constant_dynamic-slice_fusion.1), channel_id=1, source_target_pairs={{0,16},{2,18},{4,20},{6,22},{8,24},{10,26},{12,28},{14,30},{16,0},... | collective-permute-start | bytes 786440 | tf_op jit(solution)/shard_map/ppermute | solution.py:188
  130.9 12.3 %collective-permute-start.13 = (bf16[128,1024]{1,0:T(8,128)(2,1)S(1)}, bf16[128,1024]{1,0:T(8,128)(2,1)S(1)}, u32[]{:S(2)}, u32[]{:S(2)}) collective-permute-start(bf16[128,1024]{1,0:T(8,128)(2,1)S(1)} %constant_dynamic-slice_fusion.5), channel_id=1, source_target_pairs={{0,8},{2,10},{4,12},{6,14},{8,0},{10,2},{12,4},{14,6},{16,24},{18,... | collective-permute-start | bytes 786440 | tf_op jit(solution)/shard_map/ppermute | solution.py:188
  142.6 5.0 %collective-permute-start.22 = (bf16[64,1024]{1,0:T(8,128)(2,1)S(1)}, bf16[64,1024]{1,0:T(8,128)(2,1)S(1)}, u32[]{:S(2)}, u32[]{:S(2)}) collective-permute-start(bf16[64,1024]{1,0:T(8,128)(2,1)S(1)} %constant_dynamic-slice_fusion), channel_id=1, source_target_pairs={{0,4},{2,6},{4,0},{6,2},{8,12},{10,14},{12,8},{14,10},{16,20},{18,... | collective-permute-start | bytes 393224 | tf_op jit(solution)/shard_map/ppermute | solution.py:188
  143.3 9.0 %collective-permute-start.14 = (bf16[64,1024]{1,0:T(8,128)(2,1)S(1)}, bf16[64,1024]{1,0:T(8,128)(2,1)S(1)}, u32[]{:S(2)}, u32[]{:S(2)}) collective-permute-start(bf16[64,1024]{1,0:T(8,128)(2,1)S(1)} %constant_dynamic-slice_fusion.4), channel_id=1, source_target_pairs={{0,16},{2,18},{4,20},{6,22},{8,24},{10,26},{12,28},{14,30},{16,0},... | collective-permute-start | bytes 393224 | tf_op jit(solution)/shard_map/ppermute | solution.py:188
  147.7 5.0 %collective-permute-start.23 = (bf16[64,1024]{1,0:T(8,128)(2,1)S(1)}, bf16[64,1024]{1,0:T(8,128)(2,1)S(1)}, u32[]{:S(2)}, u32[]{:S(2)}) collective-permute-start(bf16[64,1024]{1,0:T(8,128)(2,1)S(1)} %add_convert_fusion.6), channel_id=1, source_target_pairs={{0,4},{2,6},{4,0},{6,2},{8,12},{10,14},{12,8},{14,10},{16,20},{18,... | collective-permute-start | bytes 393224 | tf_op jit(solution)/shard_map/ppermute | solution.py:188
  152.3 5.9 %collective-permute-start.15 = (bf16[64,1024]{1,0:T(8,128)(2,1)S(1)}, bf16[64,1024]{1,0:T(8,128)(2,1)S(1)}, u32[]{:S(2)}, u32[]{:S(2)}) collective-permute-start(bf16[64,1024]{1,0:T(8,128)(2,1)S(1)} %add_convert_fusion.7), channel_id=1, source_target_pairs={{0,16},{2,18},{4,20},{6,22},{8,24},{10,26},{12,28},{14,30},{16,0},... | collective-permute-start | bytes 393224 | tf_op jit(solution)/shard_map/ppermute | solution.py:188
  152.8 16.8 %collective-permute-start.24 = (bf16[128,1024]{1,0:T(8,128)(2,1)S(1)}, bf16[128,1024]{1,0:T(8,128)(2,1)S(1)}, u32[]{:S(2)}, u32[]{:S(2)}) collective-permute-start(bf16[128,1024]{1,0:T(8,128)(2,1)S(1)} %maximum_select_fusion.10), channel_id=1, source_target_pairs={{0,16},{2,18},{4,20},{6,22},{8,24},{10,26},{12,28},{14,30},{16,0},... | collective-permute-start | bytes 786440 | tf_op jit(solution)/shard_map/ppermute | solution.py:188
  158.3 14.5 %collective-permute-start.16 = (bf16[128,1024]{1,0:T(8,128)(2,1)S(1)}, bf16[128,1024]{1,0:T(8,128)(2,1)S(1)}, u32[]{:S(2)}, u32[]{:S(2)}) collective-permute-start(bf16[128,1024]{1,0:T(8,128)(2,1)S(1)} %maximum_select_fusion.9), channel_id=1, source_target_pairs={{0,8},{2,10},{4,12},{6,14},{8,0},{10,2},{12,4},{14,6},{16,24},{18,... | collective-permute-start | bytes 786440 | tf_op jit(solution)/shard_map/ppermute | solution.py:188
  169.7 13.1 %collective-permute-start.25 = (bf16[256,1024]{1,0:T(8,128)(2,1)S(1)}, bf16[256,1024]{1,0:T(8,128)(2,1)S(1)}, u32[]{:S(2)}, u32[]{:S(2)}) collective-permute-start(bf16[256,1024]{1,0:T(8,128)(2,1)S(1)} %maximum_select_fusion.8), channel_id=1, source_target_pairs={{0,8},{2,10},{4,12},{6,14},{8,0},{10,2},{12,4},{14,6},{16,24},{18,... | collective-permute-start | bytes 1572872 | tf_op jit(solution)/shard_map/ppermute | solution.py:188
  172.9 11.7 %collective-permute-start.17 = (bf16[256,1024]{1,0:T(8,128)(2,1)S(1)}, bf16[256,1024]{1,0:T(8,128)(2,1)}, u32[]{:S(2)}, u32[]{:S(2)}) collective-permute-start(bf16[256,1024]{1,0:T(8,128)(2,1)S(1)} %maximum_select_fusion.7), channel_id=1, source_target_pairs={{0,4},{2,6},{4,0},{6,2},{8,12},{10,14},{12,8},{14,10},{16,20},{18,... | collective-permute-start | bytes 1572872 | tf_op jit(solution)/shard_map/ppermute | solution.py:188
  183.3 28.8 %collective-permute-start.26 = (bf16[512,1024]{1,0:T(8,128)(2,1)S(1)}, bf16[512,1024]{1,0:T(8,128)(2,1)}, u32[]{:S(2)}, u32[]{:S(2)}) collective-permute-start(bf16[512,1024]{1,0:T(8,128)(2,1)S(1)} %maximum_select_fusion.6), channel_id=1, source_target_pairs={{0,2},{2,0},{4,6},{6,4},{8,10},{10,8},{12,14},{14,12},{16,18},{18,... | collective-permute-start | bytes 3145736 | tf_op jit(solution)/shard_map/ppermute | solution.py:188
  186.2 28.5 %collective-permute-start.18 = (bf16[512,1024]{1,0:T(8,128)(2,1)S(1)}, bf16[512,1024]{1,0:T(8,128)(2,1)}, u32[]{:S(2)}, u32[]{:S(2)}) collective-permute-start(bf16[512,1024]{1,0:T(8,128)(2,1)S(1)} %maximum_select_fusion.5), channel_id=1, source_target_pairs={{0,2},{2,0},{4,6},{6,4},{8,10},{10,8},{12,14},{14,12},{16,18},{18,... | collective-permute-start | bytes 3145736 | tf_op jit(solution)/shard_map/ppermute | solution.py:188
  189.4 19.6 %collective-permute-start.8 = (bf16[256,1024]{1,0:T(8,128)(2,1)}, bf16[256,1024]{1,0:T(8,128)(2,1)S(1)}, u32[]{:S(2)}, u32[]{:S(2)}) collective-permute-start(bf16[256,1024]{1,0:T(8,128)(2,1)} %fusion.13), channel_id=1, source_target_pairs={{0,1},{1,0},{2,3},{3,2},{4,5},{5,4},{6,7},{7,6},{8,9},{9,8},{10,11... | collective-permute-start | bytes 1572872 | tf_op jit(solution)/shard_map/ppermute | solution.py:302
  191.0 1.3 collective-permute-start.27
  192.3 4.0 %collective-permute-start.28 = (f32[5,1024]{1,0:T(8,128)S(1)}, f32[5,1024]{1,0:T(8,128)S(1)}, u32[]{:S(2)}, u32[]{:S(2)}) collective-permute-start(f32[5,1024]{1,0:T(8,128)S(1)} %fusion.90), channel_id=1, source_target_pairs={{0,4},{2,6},{4,0},{6,2},{8,12},{10,14},{12,8},{14,10},{16,20},{18,... | collective-permute-start | bytes 61448 | tf_op jit(solution)/shard_map/ppermute | solution.py:148
  196.2 3.9 %collective-permute-start.29 = (f32[5,1024]{1,0:T(8,128)S(1)}, f32[5,1024]{1,0:T(8,128)S(1)}, u32[]{:S(2)}, u32[]{:S(2)}) collective-permute-start(f32[5,1024]{1,0:T(8,128)S(1)} %add.290), channel_id=1, source_target_pairs={{0,8},{2,10},{4,12},{6,14},{8,0},{10,2},{12,4},{14,6},{16,24},{18,... | collective-permute-start | bytes 61448 | tf_op jit(solution)/shard_map/ppermute | solution.py:148
  200.2 7.6 %collective-permute-start.30 = (f32[5,1024]{1,0:T(8,128)S(1)}, f32[5,1024]{1,0:T(8,128)S(1)}, u32[]{:S(2)}, u32[]{:S(2)}) collective-permute-start(f32[5,1024]{1,0:T(8,128)S(1)} %add.291), channel_id=1, source_target_pairs={{0,16},{2,18},{4,20},{6,22},{8,24},{10,26},{12,28},{14,30},{16,0},... | collective-permute-start | bytes 61448 | tf_op jit(solution)/shard_map/ppermute | solution.py:148
  (29 other events, 130.9 us)

commit v3 on v2

--- a/solution.py
+++ b/solution.py
@@ -177,7 +177,7 @@
     return result
 
 
-def summed_rows(value, axis):
+def summed_rows(value, axis, beside):
     count, me = lax.axis_size(axis), lax.axis_index(axis)
     bits = [1 << b for b in range(count.bit_length() - 1)]
     orders = (bits, bits[:1] + bits[2:] + bits[1:2])
@@ -195,6 +195,7 @@
             keep = lax.dynamic_slice_in_dim(parts[p], upper * rows, rows, 0)
             send = lax.dynamic_slice_in_dim(parts[p], (1 - upper) * rows, rows, 0)
             parts[p] = (keep.astype(F32) + swapped(send, bit).astype(F32)).astype(BF16)
+    parts, beside = lax.optimization_barrier((parts, beside))
     for step in reversed(range(len(bits))):
         for p in range(2):
             bit = orders[p][step]
@@ -205,7 +206,7 @@
                 jnp.concatenate([parts[p], other], 0),
                 jnp.concatenate([other, parts[p]], 0),
             )
-    return jnp.concatenate(parts, 0)
+    return jnp.concatenate(parts, 0), beside
 
 
 def vmem_call(body, shapes, *operands):
@@ -323,7 +324,8 @@
     )
     weight_local = dot(both, grad_inner, ((0,), (0,))).astype(BF16)
     tiny = summed_whole(jnp.concatenate([filt, skip], 0), "ctx")
-    weight_grad = summed_rows(weight_local, "ctx").astype(F32)
+    weight_grad, (tiny, layer_out) = summed_rows(weight_local, "ctx", (tiny, layer_out))
+    weight_grad = weight_grad.astype(F32)
     return (layer_out, weight_grad, tiny[:taken], tiny[taken])
 
 

time: 223 us -> 207 us (0.928)
  starting transfers between devices: 52.7 us -> 41.5 us
  other arithmetic: 31.5 us -> 28.7 us
  matrix products: 21.9 us -> 19.4 us
    ppermute x16, starting transfers between devices: 22.2 us -> 8.39 us  [swapped(): return lax.ppermute(part, axis, [(i, i ^ bit) for i in range(count)])]
    ppermute x1, waiting for transfers between devices: 0.01 us -> 4.4 us  [per_device(): arrived = lax.ppermute(dot(mixed16, theirs).astype(BF16), 'ch', swap)]
    ppermute x4, waiting for transfers between devices: 10.2 us -> 5.96 us  [summed_whole(): lax.ppermute(value, axis, [(i, i ^ 1 << b) for i in range(count)])]
    ppermute x4, starting transfers between devices: 6.62 us -> 9.34 us  [summed_whole(): lax.ppermute(value, axis, [(i, i ^ 1 << b) for i in range(count)])]
    select_n x8, other arithmetic: 7.58 us -> 4.92 us  [summed_rows(): jnp.where(upper == 0, jnp.concatenate([parts[p], other], 0), jnp.concaten...]
    dot_general x7, matrix products: 21.3 us -> 18.9 us  [dot(): lax.dot_general(a, b, (dims, ((), ())), preferred_element_type=F32, preci...]
  transfers between devices with their start and end apart: 31 -> 31, of which waited for: 23 -> 24; matrix products, arithmetic and copies ran while one was open for 19% -> 17% of each run, Pallas kernels for 0% -> 0%
where the time goes in v3:
time: 207 us; the launch traced here: 206 us
  waiting for transfers between devices  83.8 us (40%)
  starting transfers between devices  41.5 us (20%)
  other arithmetic  28.7 us (14%)
  matrix products  19.4 us (9%)
  local copies, waits for them, and re-layouts  15.9 us (8%)
  Pallas kernels  15.5 us (7%)
    ppermute x16, waiting for transfers between devices, swapped(): return lax.ppermute(part, axis, [(i, i ^ bit) for i in range(count)])  50.3 us
    dot_general x7, matrix products, dot(): lax.dot_general(a, b, (dims, ((), ())), preferred_element_type=F32, preci...  18.9 us
    pallas_call x2, Pallas kernels, vmem_call(): pl.pallas_call(body, out_shape=[jax.ShapeDtypeStruct(*s) for s in shapes]...  15.5 us
    ppermute x2, waiting for transfers between devices, gathered(): other = lax.ppermute(part, 'ch', swap)  12.2 us
    ppermute x4, starting transfers between devices, entering(): lax.ppermute(packed, axis, [(i, i ^ bit) for i in range(count)]).astype(F32)  9.99 us
    ppermute x4, waiting for transfers between devices, entering(): lax.ppermute(packed, axis, [(i, i ^ bit) for i in range(count)]).astype(F32)  9.53 us
    ppermute x4, starting transfers between devices, summed_whole(): lax.ppermute(value, axis, [(i, i ^ 1 << b) for i in range(count)])  9.34 us
    ppermute x16, starting transfers between devices, swapped(): return lax.ppermute(part, axis, [(i, i ^ bit) for i in range(count)])  8.39 us
  transfers between devices with their start and end apart: 31, of which 24 were waited for; matrix products, arithmetic and copies ran while one was open for 17% of the time, Pallas kernels for 0%

profile of v3, /device:TPU:0, one launch (start us, length us, event | category | flops | bytes accessed | tf_op | source)
XLA Modules:
  0.0 206.2 jit_solution(15528119753508464086)
XLA Ops:
  0.6 3.0 %collective-permute-start = (bf16[256,1024]{1,0:T(8,128)(2,1)}, bf16[256,1024]{1,0:T(8,128)(2,1)S(1)}, u32[]{:S(2)}, u32[]{:S(2)}) collective-permute-start(bf16[256,1024]{1,0:T(8,128)(2,1)} %param.12), channel_id=1, source_target_pairs={{0,1},{1,0},{2,3},{3,2},{4,5},{5,4},{6,7},{7,6},{8,9},{9,8},{10,11... | collective-permute-start | bytes 1572872 | tf_op jit(solution)/shard_map/ppermute | solution.py:244
  4.5 12.2 %collective-permute-done = bf16[256,1024]{1,0:T(8,128)(2,1)S(1)} collective-permute-done((bf16[256,1024]{1,0:T(8,128)(2,1)}, bf16[256,1024]{1,0:T(8,128)(2,1)S(1)}, u32[]{:S(2)}, u32[]{:S(2)}) %collective-permute-start) | collective-permute-done | bytes 524320 | tf_op jit(solution)/shard_map/ppermute | solution.py:244
  18.3 3.4 %fusion.2 = bf16[256,2048]{1,0:T(8,128)(2,1)S(1)} fusion(bf16[256,2048]{1,0:T(8,128)(2,1)S(1)} %maximum_select_fusion.2, s32[2048]{0:T(1024)S(1)} %copy-done.29), kind=kOutput, calls=%fused_computation.5 | convolution fusion | flops 2152202240 | bytes 2105344 | tf_op jit(solution)/shard_map/dot_general | solution.py:16
  23.2 5.0 %convolution_convert_fusion.1 = bf16[512,1024]{1,0:T(8,128)(2,1)S(1)} fusion(bf16[2048,1024]{1,0:T(8,128)(2,1)} %param.14, bf16[256,2048]{1,0:T(8,128)(2,1)} %copy-done.30, bf16[256,2048]{1,0:T(8,128)(2,1)S(1)} %maximum_select_fusion.2), kind=kOutput, calls=%fused_computation.15 | convolution fusion | flops 2152202240 | bytes 7340032 | tf_op jit(solution)/shard_map/dot_general | solution.py:16
  30.8 3.6 %fusion.16.back = f32[256,1024]{1,0:T(8,128)} fusion(bf16[1024,2048]{1,0:T(8,128)(2,1)S(1)} %copy-done.24, bf16[256,1024]{1,0:T(8,128)(2,1)} %collective-permute-done.3, bf16[256,1024]{1,0:T(8,128)(2,1)S(1)} %copy-done.26, pred[]{:T(512)S(6)} %eq.85), kind=kOutput, calls=%fused_computation.21 | convolution fusion | flops 1078460416 | bytes 6291457 | tf_op jit(solution)/shard_map/dot_general | solution.py:16
  34.5 3.3 %collective-permute-start.1 = (bf16[16,1024]{1,0:T(8,128)(2,1)S(1)}, bf16[16,1024]{1,0:T(8,128)(2,1)S(1)}, u32[]{:S(2)}, u32[]{:S(2)}) collective-permute-start(bf16[16,1024]{1,0:T(8,128)(2,1)S(1)} %get-tuple-element.49), channel_id=1, source_target_pairs={{0,2},{2,4},{4,6},{6,8},{8,10},{10,12},{12,14},{14,16},{16,18},{18... | collective-permute-start | bytes 98312 | tf_op jit(solution)/shard_map/ppermute | solution.py:259
  38.6 9.5 %shard_map.147 = (f32[256,1024]{1,0:T(8,128)S(1)}, f32[2,256,1024]{2,1,0:T(8,128)}, f32[2,256,1024]{2,1,0:T(8,128)}, bf16[4,16,1024]{2,1,0:T(8,128)(2,1)S(1)}, f32[1,1024]{1,0:T(1,128)S(1)}) custom-call(bf16[272,1024]{1,0:T(8,128)(2,1)S(1)} %pad_maximum_fusion.4.xf, bf16[272,1024]{1,0:T(8,128)(2,1)S(1)} %pad_maximum_fusion.5.xr, f32[256,1024]{1,0:T(8,128)S(1)} %copy-done, ...), custom_call_target="tpu_custom_call" | custom-call | tf_op jit(solution)/shard_map/pallas_call | solution.py:214
  53.7 2.6 %collective-permute-start.5 = (bf16[80,1024]{1,0:T(8,128)(2,1)}, bf16[80,1024]{1,0:T(8,128)(2,1)S(1)}, u32[]{:S(2)}, u32[]{:S(2)}) collective-permute-start(bf16[80,1024]{1,0:T(8,128)(2,1)} %pad_maximum_fusion.7), channel_id=1, source_target_pairs={{0,4},{2,6},{4,0},{6,2},{8,12},{10,14},{12,8},{14,10},{16,20},{18,... | collective-permute-start | bytes 491528 | tf_op jit(solution)/shard_map/ppermute | solution.py:165
  68.7 2.7 %collective-permute-start.6 = (bf16[80,1024]{1,0:T(8,128)(2,1)}, bf16[80,1024]{1,0:T(8,128)(2,1)S(1)}, u32[]{:S(2)}, u32[]{:S(2)}) collective-permute-start(bf16[80,1024]{1,0:T(8,128)(2,1)} %pad_maximum_fusion.8), channel_id=1, source_target_pairs={{0,8},{2,10},{4,12},{6,14},{8,0},{10,2},{12,4},{14,6},{16,24},{18,... | collective-permute-start | bytes 491528 | tf_op jit(solution)/shard_map/ppermute | solution.py:165
  81.3 2.8 %collective-permute-start.7 = (bf16[80,1024]{1,0:T(8,128)(2,1)S(1)}, bf16[80,1024]{1,0:T(8,128)(2,1)S(1)}, u32[]{:S(2)}, u32[]{:S(2)}) collective-permute-start(bf16[80,1024]{1,0:T(8,128)(2,1)S(1)} %pad_maximum_fusion.9), channel_id=1, source_target_pairs={{0,16},{2,18},{4,20},{6,22},{8,24},{10,26},{12,28},{14,30},{16,0},... | collective-permute-start | bytes 491528 | tf_op jit(solution)/shard_map/ppermute | solution.py:165
  84.1 6.4 %collective-permute-done.7 = bf16[80,1024]{1,0:T(8,128)(2,1)S(1)} collective-permute-done((bf16[80,1024]{1,0:T(8,128)(2,1)S(1)}, bf16[80,1024]{1,0:T(8,128)(2,1)S(1)}, u32[]{:S(2)}, u32[]{:S(2)}) %collective-permute-start.7) | collective-permute-done | bytes 163872 | tf_op jit(solution)/shard_map/ppermute | solution.py:165
  90.8 6.0 %shard_map.148 = (bf16[256,1024]{1,0:T(8,128)(2,1)S(1)}, bf16[512,1024]{1,0:T(8,128)(2,1)S(1)}, f32[2,8,1024]{2,1,0:T(8,128)S(1)}, f32[2,8,1024]{2,1,0:T(8,128)S(1)}, f32[4,1024]{1,0:T(4,128)S(1)}) custom-call(bf16[272,1024]{1,0:T(8,128)(2,1)S(1)} %pad_maximum_fusion.4.xf, bf16[272,1024]{1,0:T(8,128)(2,1)S(1)} %pad_maximum_fusion.5.xr, ...), custom_call_target="tpu_custom_call" | custom-call | tf_op jit(solution)/shard_map/pallas_call | solution.py:214
  98.2 3.0 %collective-permute-start.9 = (f32[8,1024]{1,0:T(8,128)S(1)}, f32[8,1024]{1,0:T(8,128)S(1)}, u32[]{:S(2)}, u32[]{:S(2)}) collective-permute-start(f32[8,1024]{1,0:T(8,128)S(1)} %get-tuple-element.57), channel_id=1, source_target_pairs={{0,2},{2,4},{4,6},{6,8},{8,10},{10,12},{12,14},{14,16},{16,18},{18... | collective-permute-start | bytes 98312 | tf_op jit(solution)/shard_map/ppermute | solution.py:298
  102.2 2.4 %convolution_convert_fusion = bf16[2048,1024]{1,0:T(8,128)(2,1)S(1)} fusion(bf16[248,1024]{1,0:T(8,128)(2,1)S(1)} %get-tuple-element.45, bf16[8,1024]{1,0:T(8,128)(2,1)S(1)} %get-tuple-element.55, bf16[8,1024]{1,0:T(8,128)(2,1)S(1)} %get-tuple-element.54, bf16[248,1024]{1,0:T(8,128)(2,1)S(1)} %get-tuple-element.44, bf16[256,2048]{1,0:T(8,128)(2,1)S(1)} %copy-done.31, ...), kind=kOutput, calls=%fused_computation.4 | convolution fusion | flops 2157969408 | bytes 7340032 | tf_op jit(solution)/shard_map/dot_general | solution.py:16
  108.3 2.2 %collective-permute-done.18 = f32[5,1024]{1,0:T(8,128)S(1)} collective-permute-done((f32[5,1024]{1,0:T(8,128)S(1)}, f32[5,1024]{1,0:T(8,128)S(1)}, u32[]{:S(2)}, u32[]{:S(2)}) %collective-permute-start.18) | collective-permute-done | bytes 20512 | tf_op jit(solution)/shard_map/ppermute | solution.py:148
  110.5 2.6 %collective-permute-start.19 = (f32[5,1024]{1,0:T(8,128)S(1)}, f32[5,1024]{1,0:T(8,128)S(1)}, u32[]{:S(2)}, u32[]{:S(2)}) collective-permute-start(f32[5,1024]{1,0:T(8,128)S(1)} %fusion.90), channel_id=1, source_target_pairs={{0,4},{2,6},{4,0},{6,2},{8,12},{10,14},{12,8},{14,10},{16,20},{18,... | collective-permute-start | bytes 61448 | tf_op jit(solution)/shard_map/ppermute | solution.py:148
  115.0 2.8 %collective-permute-start.20 = (f32[5,1024]{1,0:T(8,128)S(1)}, f32[5,1024]{1,0:T(8,128)S(1)}, u32[]{:S(2)}, u32[]{:S(2)}) collective-permute-start(f32[5,1024]{1,0:T(8,128)S(1)} %add.287), channel_id=1, source_target_pairs={{0,8},{2,10},{4,12},{6,14},{8,0},{10,2},{12,4},{14,6},{16,24},{18,... | collective-permute-start | bytes 61448 | tf_op jit(solution)/shard_map/ppermute | solution.py:148
  119.7 3.4 %collective-permute-start.21 = (f32[5,1024]{1,0:T(8,128)S(1)}, f32[5,1024]{1,0:T(8,128)S(1)}, u32[]{:S(2)}, u32[]{:S(2)}) collective-permute-start(f32[5,1024]{1,0:T(8,128)S(1)} %add.288), channel_id=1, source_target_pairs={{0,16},{2,18},{4,20},{6,22},{8,24},{10,26},{12,28},{14,30},{16,0},... | collective-permute-start | bytes 61448 | tf_op jit(solution)/shard_map/ppermute | solution.py:148
  123.1 2.3 %fusion.13 = bf16[256,1024]{1,0:T(8,128)(2,1)S(1)} fusion(bf16[256,1024]{1,0:T(8,128)(2,1)S(1)} %copy-done.4, bf16[1024,2048]{1,0:T(8,128)(2,1)} %param.21, s32[]{:T(128)S(6)} %select_n.359), kind=kOutput, calls=%fused_computation.18 | convolution fusion | flops 537133056 | bytes 3145732 | tf_op jit(solution)/shard_map/dot_general | solution.py:16
  130.6 2.1 %collective-permute-start.15 = (bf16[256,1024]{1,0:T(8,128)(2,1)S(1)}, bf16[256,1024]{1,0:T(8,128)(2,1)S(1)}, u32[]{:S(2)}, u32[]{:S(2)}) collective-permute-start(bf16[256,1024]{1,0:T(8,128)(2,1)S(1)} %constant_dynamic-slice_fusion.2), channel_id=1, source_target_pairs={{0,8},{2,10},{4,12},{6,14},{8,0},{10,2},{12,4},{14,6},{16,24},{18,... | collective-permute-start | bytes 1572872 | tf_op jit(solution)/shard_map/ppermute | solution.py:188
  132.7 4.4 %collective-permute-done.22 = bf16[256,1024]{1,0:T(8,128)(2,1)S(1)} collective-permute-done((bf16[256,1024]{1,0:T(8,128)(2,1)S(1)}, bf16[256,1024]{1,0:T(8,128)(2,1)S(1)}, u32[]{:S(2)}, u32[]{:S(2)}) %collective-permute-start.22) | collective-permute-done | bytes 524320 | tf_op jit(solution)/shard_map/ppermute | solution.py:303
  142.2 5.0 %collective-permute-done.15 = bf16[256,1024]{1,0:T(8,128)(2,1)S(1)} collective-permute-done((bf16[256,1024]{1,0:T(8,128)(2,1)S(1)}, bf16[256,1024]{1,0:T(8,128)(2,1)S(1)}, u32[]{:S(2)}, u32[]{:S(2)}) %collective-permute-start.15) | collective-permute-done | bytes 524320 | tf_op jit(solution)/shard_map/ppermute | solution.py:188
  147.6 2.9 %collective-permute-done.12 = bf16[128,1024]{1,0:T(8,128)(2,1)S(1)} collective-permute-done((bf16[128,1024]{1,0:T(8,128)(2,1)S(1)}, bf16[128,1024]{1,0:T(8,128)(2,1)S(1)}, u32[]{:S(2)}, u32[]{:S(2)}) %collective-permute-start.12) | collective-permute-done | bytes 262176 | tf_op jit(solution)/shard_map/ppermute | solution.py:188
  151.0 9.7 %collective-permute-done.16 = bf16[128,1024]{1,0:T(8,128)(2,1)S(1)} collective-permute-done((bf16[128,1024]{1,0:T(8,128)(2,1)S(1)}, bf16[128,1024]{1,0:T(8,128)(2,1)S(1)}, u32[]{:S(2)}, u32[]{:S(2)}) %collective-permute-start.16) | collective-permute-done | bytes 262176 | tf_op jit(solution)/shard_map/ppermute | solution.py:188
  162.2 3.7 %collective-permute-done.17 = bf16[64,1024]{1,0:T(8,128)(2,1)S(1)} collective-permute-done((bf16[64,1024]{1,0:T(8,128)(2,1)S(1)}, bf16[64,1024]{1,0:T(8,128)(2,1)S(1)}, u32[]{:S(2)}, u32[]{:S(2)}) %collective-permute-start.17) | collective-permute-done | bytes 131104 | tf_op jit(solution)/shard_map/ppermute | solution.py:188
  167.0 4.0 %collective-permute-done.27 = bf16[64,1024]{1,0:T(8,128)(2,1)S(1)} collective-permute-done((bf16[64,1024]{1,0:T(8,128)(2,1)S(1)}, bf16[64,1024]{1,0:T(8,128)(2,1)S(1)}, u32[]{:S(2)}, u32[]{:S(2)}) %collective-permute-start.27) | collective-permute-done | bytes 131104 | tf_op jit(solution)/shard_map/ppermute | solution.py:188
  171.1 3.6 %collective-permute-done.23 = bf16[64,1024]{1,0:T(8,128)(2,1)S(1)} collective-permute-done((bf16[64,1024]{1,0:T(8,128)(2,1)S(1)}, bf16[64,1024]{1,0:T(8,128)(2,1)S(1)}, u32[]{:S(2)}, u32[]{:S(2)}) %collective-permute-start.23) | collective-permute-done | bytes 131104 | tf_op jit(solution)/shard_map/ppermute | solution.py:188
  174.9 6.0 %collective-permute-done.28 = bf16[128,1024]{1,0:T(8,128)(2,1)S(1)} collective-permute-done((bf16[128,1024]{1,0:T(8,128)(2,1)S(1)}, bf16[128,1024]{1,0:T(8,128)(2,1)S(1)}, u32[]{:S(2)}, u32[]{:S(2)}) %collective-permute-start.28) | collective-permute-done | bytes 262176 | tf_op jit(solution)/shard_map/ppermute | solution.py:188
  181.1 5.2 %collective-permute-done.24 = bf16[128,1024]{1,0:T(8,128)(2,1)S(1)} collective-permute-done((bf16[128,1024]{1,0:T(8,128)(2,1)S(1)}, bf16[128,1024]{1,0:T(8,128)(2,1)S(1)}, u32[]{:S(2)}, u32[]{:S(2)}) %collective-permute-start.24) | collective-permute-done | bytes 262176 | tf_op jit(solution)/shard_map/ppermute | solution.py:188
  187.3 6.4 %collective-permute-done.29 = bf16[256,1024]{1,0:T(8,128)(2,1)S(1)} collective-permute-done((bf16[256,1024]{1,0:T(8,128)(2,1)S(1)}, bf16[256,1024]{1,0:T(8,128)(2,1)S(1)}, u32[]{:S(2)}, u32[]{:S(2)}) %collective-permute-start.29) | collective-permute-done | bytes 524320 | tf_op jit(solution)/shard_map/ppermute | solution.py:188
  199.1 2.6 %maximum_select_fusion = bf16[1024,1024]{1,0:T(8,128)(2,1)S(1)} fusion(bf16[512,1024]{1,0:T(8,128)(2,1)} %collective-permute-done.26, bf16[512,1024]{1,0:T(8,128)(2,1)S(1)} %maximum_select_fusion.5, pred[]{:T(512)S(6)} %eq.100), kind=kLoop, calls=%fused_computation.7 | loop fusion | flops 9437184 | bytes 4194305 | tf_op jit(solution)/shard_map/jit(_where)/select_n | solution.py:204
  201.7 4.5 %maximum_convert_fusion = f32[2048,1024]{1,0:T(8,128)} fusion(bf16[1024,1024]{1,0:T(8,128)(2,1)S(1)} %maximum_select_fusion.1, bf16[1024,1024]{1,0:T(8,128)(2,1)S(1)} %maximum_select_fusion), kind=kLoop, calls=%fused_computation.3 | loop fusion | flops 8388608 | bytes 12582912 | tf_op jit(solution)/shard_map/convert_element_type | solution.py:328
  (195 shorter events, 65.3 us)
Async XLA Ops:
  0.6 16.0 %collective-permute-start = (bf16[256,1024]{1,0:T(8,128)(2,1)}, bf16[256,1024]{1,0:T(8,128)(2,1)S(1)}, u32[]{:S(2)}, u32[]{:S(2)}) collective-permute-start(bf16[256,1024]{1,0:T(8,128)(2,1)} %param.12), channel_id=1, source_target_pairs={{0,1},{1,0},{2,3},{3,2},{4,5},{5,4},{6,7},{7,6},{8,9},{9,8},{10,11... | collective-permute-start | bytes 1572872 | tf_op jit(solution)/shard_map/ppermute | solution.py:244
  3.7 27.1 %collective-permute-start.3 = (bf16[256,1024]{1,0:T(8,128)(2,1)}, bf16[256,1024]{1,0:T(8,128)(2,1)}, u32[]{:S(2)}, u32[]{:S(2)}) collective-permute-start(bf16[256,1024]{1,0:T(8,128)(2,1)} %param.22), channel_id=1, source_target_pairs={{0,1},{1,0},{2,3},{3,2},{4,5},{5,4},{6,7},{7,6},{8,9},{9,8},{10,11... | collective-permute-start | bytes 1572872 | tf_op jit(solution)/shard_map/ppermute | solution.py:244
  28.8 9.1 %collective-permute-start.2 = (bf16[16,1024]{1,0:T(8,128)(2,1)S(1)}, bf16[16,1024]{1,0:T(8,128)(2,1)S(1)}, u32[]{:S(2)}, u32[]{:S(2)}) collective-permute-start(bf16[16,1024]{1,0:T(8,128)(2,1)S(1)} %get-tuple-element.48), channel_id=1, source_target_pairs={{2,0},{4,2},{6,4},{8,6},{10,8},{12,10},{14,12},{16,14},{18,16},{20... | collective-permute-start | bytes 98312 | tf_op jit(solution)/shard_map/ppermute | solution.py:260
  34.5 4.0 %collective-permute-start.1 = (bf16[16,1024]{1,0:T(8,128)(2,1)S(1)}, bf16[16,1024]{1,0:T(8,128)(2,1)S(1)}, u32[]{:S(2)}, u32[]{:S(2)}) collective-permute-start(bf16[16,1024]{1,0:T(8,128)(2,1)S(1)} %get-tuple-element.49), channel_id=1, source_target_pairs={{0,2},{2,4},{4,6},{6,8},{8,10},{10,12},{12,14},{14,16},{16,18},{18... | collective-permute-start | bytes 98312 | tf_op jit(solution)/shard_map/ppermute | solution.py:259
  48.2 2.9 %collective-permute-start.4 = (bf16[80,1024]{1,0:T(8,128)(2,1)S(1)}, bf16[80,1024]{1,0:T(8,128)(2,1)S(1)}, u32[]{:S(2)}, u32[]{:S(2)}) collective-permute-start(bf16[80,1024]{1,0:T(8,128)(2,1)S(1)} %pad_maximum_fusion.6), channel_id=1, source_target_pairs={{0,2},{2,0},{4,6},{6,4},{8,10},{10,8},{12,14},{14,12},{16,18},{18,... | collective-permute-start | bytes 491528 | tf_op jit(solution)/shard_map/ppermute | solution.py:165
  53.7 7.3 %collective-permute-start.5 = (bf16[80,1024]{1,0:T(8,128)(2,1)}, bf16[80,1024]{1,0:T(8,128)(2,1)S(1)}, u32[]{:S(2)}, u32[]{:S(2)}) collective-permute-start(bf16[80,1024]{1,0:T(8,128)(2,1)} %pad_maximum_fusion.7), channel_id=1, source_target_pairs={{0,4},{2,6},{4,0},{6,2},{8,12},{10,14},{12,8},{14,10},{16,20},{18,... | collective-permute-start | bytes 491528 | tf_op jit(solution)/shard_map/ppermute | solution.py:165
  68.7 6.6 %collective-permute-start.6 = (bf16[80,1024]{1,0:T(8,128)(2,1)}, bf16[80,1024]{1,0:T(8,128)(2,1)S(1)}, u32[]{:S(2)}, u32[]{:S(2)}) collective-permute-start(bf16[80,1024]{1,0:T(8,128)(2,1)} %pad_maximum_fusion.8), channel_id=1, source_target_pairs={{0,8},{2,10},{4,12},{6,14},{8,0},{10,2},{12,4},{14,6},{16,24},{18,... | collective-permute-start | bytes 491528 | tf_op jit(solution)/shard_map/ppermute | solution.py:165
  81.3 9.3 %collective-permute-start.7 = (bf16[80,1024]{1,0:T(8,128)(2,1)S(1)}, bf16[80,1024]{1,0:T(8,128)(2,1)S(1)}, u32[]{:S(2)}, u32[]{:S(2)}) collective-permute-start(bf16[80,1024]{1,0:T(8,128)(2,1)S(1)} %pad_maximum_fusion.9), channel_id=1, source_target_pairs={{0,16},{2,18},{4,20},{6,22},{8,24},{10,26},{12,28},{14,30},{16,0},... | collective-permute-start | bytes 491528 | tf_op jit(solution)/shard_map/ppermute | solution.py:165
  96.8 4.5 %collective-permute-start.8 = (f32[8,1024]{1,0:T(8,128)S(1)}, f32[8,1024]{1,0:T(8,128)S(1)}, u32[]{:S(2)}, u32[]{:S(2)}) collective-permute-start(f32[8,1024]{1,0:T(8,128)S(1)} %get-tuple-element.56), channel_id=1, source_target_pairs={{2,0},{4,2},{6,4},{8,6},{10,8},{12,10},{14,12},{16,14},{18,16},{20... | collective-permute-start | bytes 98312 | tf_op jit(solution)/shard_map/ppermute | solution.py:297
  98.2 3.9 %collective-permute-start.9 = (f32[8,1024]{1,0:T(8,128)S(1)}, f32[8,1024]{1,0:T(8,128)S(1)}, u32[]{:S(2)}, u32[]{:S(2)}) collective-permute-start(f32[8,1024]{1,0:T(8,128)S(1)} %get-tuple-element.57), channel_id=1, source_target_pairs={{0,2},{2,4},{4,6},{6,8},{8,10},{10,12},{12,14},{14,16},{16,18},{18... | collective-permute-start | bytes 98312 | tf_op jit(solution)/shard_map/ppermute | solution.py:298
  105.0 18.0 %copy-start.4 = (bf16[256,1024]{1,0:T(8,128)(2,1)S(1)}, bf16[256,1024]{1,0:T(8,128)(2,1)}, u32[]{:S(2)}) copy-start(bf16[256,1024]{1,0:T(8,128)(2,1)} %copy-done.3) | copy-start | bytes 1572868
  106.1 20.8 %collective-permute-start.10 = (bf16[512,1024]{1,0:T(8,128)(2,1)}, bf16[512,1024]{1,0:T(8,128)(2,1)}, u32[]{:S(2)}, u32[]{:S(2)}) collective-permute-start(bf16[512,1024]{1,0:T(8,128)(2,1)} %constant_dynamic-slice_fusion.7), channel_id=1, source_target_pairs={{0,2},{2,0},{4,6},{6,4},{8,10},{10,8},{12,14},{14,12},{16,18},{18,... | collective-permute-start | bytes 3145736 | tf_op jit(solution)/shard_map/ppermute | solution.py:188
  107.7 21.1 %collective-permute-start.14 = (bf16[512,1024]{1,0:T(8,128)(2,1)}, bf16[512,1024]{1,0:T(8,128)(2,1)}, u32[]{:S(2)}, u32[]{:S(2)}) collective-permute-start(bf16[512,1024]{1,0:T(8,128)(2,1)} %constant_dynamic-slice_fusion.3), channel_id=1, source_target_pairs={{0,2},{2,0},{4,6},{6,4},{8,10},{10,8},{12,14},{14,12},{16,18},{18,... | collective-permute-start | bytes 3145736 | tf_op jit(solution)/shard_map/ppermute | solution.py:188
  107.7 2.7 %collective-permute-start.18 = (f32[5,1024]{1,0:T(8,128)S(1)}, f32[5,1024]{1,0:T(8,128)S(1)}, u32[]{:S(2)}, u32[]{:S(2)}) collective-permute-start(f32[5,1024]{1,0:T(8,128)S(1)} %pad_maximum_fusion.10), channel_id=1, source_target_pairs={{0,2},{2,0},{4,6},{6,4},{8,10},{10,8},{12,14},{14,12},{16,18},{18,... | collective-permute-start | bytes 61448 | tf_op jit(solution)/shard_map/ppermute | solution.py:148
  110.5 4.5 %collective-permute-start.19 = (f32[5,1024]{1,0:T(8,128)S(1)}, f32[5,1024]{1,0:T(8,128)S(1)}, u32[]{:S(2)}, u32[]{:S(2)}) collective-permute-start(f32[5,1024]{1,0:T(8,128)S(1)} %fusion.90), channel_id=1, source_target_pairs={{0,4},{2,6},{4,0},{6,2},{8,12},{10,14},{12,8},{14,10},{16,20},{18,... | collective-permute-start | bytes 61448 | tf_op jit(solution)/shard_map/ppermute | solution.py:148
  115.0 4.7 %collective-permute-start.20 = (f32[5,1024]{1,0:T(8,128)S(1)}, f32[5,1024]{1,0:T(8,128)S(1)}, u32[]{:S(2)}, u32[]{:S(2)}) collective-permute-start(f32[5,1024]{1,0:T(8,128)S(1)} %add.287), channel_id=1, source_target_pairs={{0,8},{2,10},{4,12},{6,14},{8,0},{10,2},{12,4},{14,6},{16,24},{18,... | collective-permute-start | bytes 61448 | tf_op jit(solution)/shard_map/ppermute | solution.py:148
  119.7 7.3 %collective-permute-start.21 = (f32[5,1024]{1,0:T(8,128)S(1)}, f32[5,1024]{1,0:T(8,128)S(1)}, u32[]{:S(2)}, u32[]{:S(2)}) collective-permute-start(f32[5,1024]{1,0:T(8,128)S(1)} %add.288), channel_id=1, source_target_pairs={{0,16},{2,18},{4,20},{6,22},{8,24},{10,26},{12,28},{14,30},{16,0},... | collective-permute-start | bytes 61448 | tf_op jit(solution)/shard_map/ppermute | solution.py:148
  125.4 11.7 %collective-permute-start.22 = (bf16[256,1024]{1,0:T(8,128)(2,1)S(1)}, bf16[256,1024]{1,0:T(8,128)(2,1)S(1)}, u32[]{:S(2)}, u32[]{:S(2)}) collective-permute-start(bf16[256,1024]{1,0:T(8,128)(2,1)S(1)} %fusion.13), channel_id=1, source_target_pairs={{0,1},{1,0},{2,3},{3,2},{4,5},{5,4},{6,7},{7,6},{8,9},{9,8},{10,11... | collective-permute-start | bytes 1572872 | tf_op jit(solution)/shard_map/ppermute | solution.py:303
  128.7 11.4 %collective-permute-start.11 = (bf16[256,1024]{1,0:T(8,128)(2,1)S(1)}, bf16[256,1024]{1,0:T(8,128)(2,1)S(1)}, u32[]{:S(2)}, u32[]{:S(2)}) collective-permute-start(bf16[256,1024]{1,0:T(8,128)(2,1)S(1)} %constant_dynamic-slice_fusion.6), channel_id=1, source_target_pairs={{0,4},{2,6},{4,0},{6,2},{8,12},{10,14},{12,8},{14,10},{16,20},{18,... | collective-permute-start | bytes 1572872 | tf_op jit(solution)/shard_map/ppermute | solution.py:188
  130.6 16.6 %collective-permute-start.15 = (bf16[256,1024]{1,0:T(8,128)(2,1)S(1)}, bf16[256,1024]{1,0:T(8,128)(2,1)S(1)}, u32[]{:S(2)}, u32[]{:S(2)}) collective-permute-start(bf16[256,1024]{1,0:T(8,128)(2,1)S(1)} %constant_dynamic-slice_fusion.2), channel_id=1, source_target_pairs={{0,8},{2,10},{4,12},{6,14},{8,0},{10,2},{12,4},{14,6},{16,24},{18,... | collective-permute-start | bytes 1572872 | tf_op jit(solution)/shard_map/ppermute | solution.py:188
  140.4 10.1 %collective-permute-start.12 = (bf16[128,1024]{1,0:T(8,128)(2,1)S(1)}, bf16[128,1024]{1,0:T(8,128)(2,1)S(1)}, u32[]{:S(2)}, u32[]{:S(2)}) collective-permute-start(bf16[128,1024]{1,0:T(8,128)(2,1)S(1)} %constant_dynamic-slice_fusion.5), channel_id=1, source_target_pairs={{0,8},{2,10},{4,12},{6,14},{8,0},{10,2},{12,4},{14,6},{16,24},{18,... | collective-permute-start | bytes 786440 | tf_op jit(solution)/shard_map/ppermute | solution.py:188
  147.5 13.3 %collective-permute-start.16 = (bf16[128,1024]{1,0:T(8,128)(2,1)S(1)}, bf16[128,1024]{1,0:T(8,128)(2,1)S(1)}, u32[]{:S(2)}, u32[]{:S(2)}) collective-permute-start(bf16[128,1024]{1,0:T(8,128)(2,1)S(1)} %constant_dynamic-slice_fusion.1), channel_id=1, source_target_pairs={{0,16},{2,18},{4,20},{6,22},{8,24},{10,26},{12,28},{14,30},{16,0},... | collective-permute-start | bytes 786440 | tf_op jit(solution)/shard_map/ppermute | solution.py:188
  150.6 11.6 %collective-permute-start.13 = (bf16[64,1024]{1,0:T(8,128)(2,1)S(1)}, bf16[64,1024]{1,0:T(8,128)(2,1)S(1)}, u32[]{:S(2)}, u32[]{:S(2)}) collective-permute-start(bf16[64,1024]{1,0:T(8,128)(2,1)S(1)} %constant_dynamic-slice_fusion.4), channel_id=1, source_target_pairs={{0,16},{2,18},{4,20},{6,22},{8,24},{10,26},{12,28},{14,30},{16,0},... | collective-permute-start | bytes 393224 | tf_op jit(solution)/shard_map/ppermute | solution.py:188
  160.9 5.0 %collective-permute-start.17 = (bf16[64,1024]{1,0:T(8,128)(2,1)S(1)}, bf16[64,1024]{1,0:T(8,128)(2,1)S(1)}, u32[]{:S(2)}, u32[]{:S(2)}) collective-permute-start(bf16[64,1024]{1,0:T(8,128)(2,1)S(1)} %constant_dynamic-slice_fusion), channel_id=1, source_target_pairs={{0,4},{2,6},{4,0},{6,2},{8,12},{10,14},{12,8},{14,10},{16,20},{18,... | collective-permute-start | bytes 393224 | tf_op jit(solution)/shard_map/ppermute | solution.py:188
  165.9 5.0 %collective-permute-start.27 = (bf16[64,1024]{1,0:T(8,128)(2,1)S(1)}, bf16[64,1024]{1,0:T(8,128)(2,1)S(1)}, u32[]{:S(2)}, u32[]{:S(2)}) collective-permute-start(bf16[64,1024]{1,0:T(8,128)(2,1)S(1)} %add_convert_fusion.6), channel_id=1, source_target_pairs={{0,4},{2,6},{4,0},{6,2},{8,12},{10,14},{12,8},{14,10},{16,20},{18,... | collective-permute-start | bytes 393224 | tf_op jit(solution)/shard_map/ppermute | solution.py:188
  167.0 7.8 %collective-permute-start.23 = (bf16[64,1024]{1,0:T(8,128)(2,1)S(1)}, bf16[64,1024]{1,0:T(8,128)(2,1)S(1)}, u32[]{:S(2)}, u32[]{:S(2)}) collective-permute-start(bf16[64,1024]{1,0:T(8,128)(2,1)S(1)} %add_convert_fusion.7), channel_id=1, source_target_pairs={{0,16},{2,18},{4,20},{6,22},{8,24},{10,26},{12,28},{14,30},{16,0},... | collective-permute-start | bytes 393224 | tf_op jit(solution)/shard_map/ppermute | solution.py:188
  171.0 9.9 %collective-permute-start.28 = (bf16[128,1024]{1,0:T(8,128)(2,1)S(1)}, bf16[128,1024]{1,0:T(8,128)(2,1)S(1)}, u32[]{:S(2)}, u32[]{:S(2)}) collective-permute-start(bf16[128,1024]{1,0:T(8,128)(2,1)S(1)} %maximum_select_fusion.10), channel_id=1, source_target_pairs={{0,16},{2,18},{4,20},{6,22},{8,24},{10,26},{12,28},{14,30},{16,0},... | collective-permute-start | bytes 786440 | tf_op jit(solution)/shard_map/ppermute | solution.py:188
  174.8 11.6 %collective-permute-start.24 = (bf16[128,1024]{1,0:T(8,128)(2,1)S(1)}, bf16[128,1024]{1,0:T(8,128)(2,1)S(1)}, u32[]{:S(2)}, u32[]{:S(2)}) collective-permute-start(bf16[128,1024]{1,0:T(8,128)(2,1)S(1)} %maximum_select_fusion.9), channel_id=1, source_target_pairs={{0,8},{2,10},{4,12},{6,14},{8,0},{10,2},{12,4},{14,6},{16,24},{18,... | collective-permute-start | bytes 786440 | tf_op jit(solution)/shard_map/ppermute | solution.py:188
  181.0 12.7 %collective-permute-start.29 = (bf16[256,1024]{1,0:T(8,128)(2,1)S(1)}, bf16[256,1024]{1,0:T(8,128)(2,1)S(1)}, u32[]{:S(2)}, u32[]{:S(2)}) collective-permute-start(bf16[256,1024]{1,0:T(8,128)(2,1)S(1)} %maximum_select_fusion.8), channel_id=1, source_target_pairs={{0,8},{2,10},{4,12},{6,14},{8,0},{10,2},{12,4},{14,6},{16,24},{18,... | collective-permute-start | bytes 1572872 | tf_op jit(solution)/shard_map/ppermute | solution.py:188
  186.5 9.2 %collective-permute-start.25 = (bf16[256,1024]{1,0:T(8,128)(2,1)S(1)}, bf16[256,1024]{1,0:T(8,128)(2,1)S(1)}, u32[]{:S(2)}, u32[]{:S(2)}) collective-permute-start(bf16[256,1024]{1,0:T(8,128)(2,1)S(1)} %maximum_select_fusion.7), channel_id=1, source_target_pairs={{0,4},{2,6},{4,0},{6,2},{8,12},{10,14},{12,8},{14,10},{16,20},{18,... | collective-permute-start | bytes 1572872 | tf_op jit(solution)/shard_map/ppermute | solution.py:188
  194.3 3.3 %collective-permute-start.30 = (bf16[512,1024]{1,0:T(8,128)(2,1)S(1)}, bf16[512,1024]{1,0:T(8,128)(2,1)S(1)}, u32[]{:S(2)}, u32[]{:S(2)}) collective-permute-start(bf16[512,1024]{1,0:T(8,128)(2,1)S(1)} %maximum_select_fusion.6), channel_id=1, source_target_pairs={{0,2},{2,0},{4,6},{6,4},{8,10},{10,8},{12,14},{14,12},{16,18},{18,... | collective-permute-start | bytes 3145736 | tf_op jit(solution)/shard_map/ppermute | solution.py:188
  196.2 2.9 %collective-permute-start.26 = (bf16[512,1024]{1,0:T(8,128)(2,1)S(1)}, bf16[512,1024]{1,0:T(8,128)(2,1)}, u32[]{:S(2)}, u32[]{:S(2)}) collective-permute-start(bf16[512,1024]{1,0:T(8,128)(2,1)S(1)} %maximum_select_fusion.5), channel_id=1, source_target_pairs={{0,2},{2,0},{4,6},{6,4},{8,10},{10,8},{12,14},{14,12},{16,18},{18,... | collective-permute-start | bytes 3145736 | tf_op jit(solution)/shard_map/ppermute | solution.py:188
  (31 other events, 166.0 us)
